TPU v7x, 512 devices: a whole 4x4x16 slice. The times are simulated.
512 devices in a mesh: ctx: 16 (over x, y), exp: 32 (over z, core).
Axes of the slice: x: 4, y: 4, z: 16, core: 2. Of those that a mesh axis runs over, the one named last changes fastest.
Arguments:
- resid: bfloat16 [2048, 3072], P('ctx', 'exp'), may hold values from -37 to 37
- queries: bfloat16 [2048, 4096], P('ctx', 'exp'), may hold values from -6 to 6
- keys: bfloat16 [2048, 4096], P('ctx', 'exp'), may hold values from -0.01171875 to 0.01171875
- values: bfloat16 [2048, 4096], P('ctx', 'exp'), may hold values from -6 to 6
- log_decay: float32 [32, 2048], P('exp', 'ctx'), may hold values from -1.5 to 0
- w_out: bfloat16 [4096, 3072], P('exp'), may hold values from -0.1875 to 0.1875
- w_up: bfloat16 [32, 3072, 6144], P('exp', None, 'ctx'), may hold values from -0.07307089 to 0.07307089
- w_down: bfloat16 [32, 6144, 3072], P('exp', 'ctx'), may hold values from -0.076546554 to 0.076546554
- expert_ids: int32 [2048, 2], P('ctx'), may hold values from 0 to 31, all different within a row; in each aligned block of 128 rows (0 to 127, 128 to 255, ...) at most 16 rows name the same one
- route_weights: float32 [2048, 2], P('ctx'), may hold values from 0.3 to 1.5
- cotangent: bfloat16 [2048, 3072], P('ctx', 'exp'), may hold values from -6 to 6
Outputs:
- layer_out: bfloat16 [2048, 3072], P('ctx', 'exp')
- resid_grad: bfloat16 [2048, 3072], P('ctx', 'exp')
- q_grad: bfloat16 [2048, 4096], P('ctx', 'exp')
- k_grad: bfloat16 [2048, 4096], P('ctx', 'exp')
- v_grad: bfloat16 [2048, 4096], P('ctx', 'exp')
Inputs may be any that keep to these rules, and one draw needn't show every extreme that they name: `expert_ids`: in each aligned block of 128 rows (the positions of one block) no expert is named by more than 16 rows; the two ids of a row differ.
All inputs are finite; a program needn't handle non-finite values.
Results may differ from a plain program's by a relative error of at most 0.02.
Values may be sent and summed in bfloat16 or wider, within the bound.
No kernel may reach another device: no remote copies, remote signals or barrier semaphores. Data moves between devices by JAX's collectives and lax.ppermute only.
A program may use at most 64 MiB of HBM per device.

v0:
```python
import jax
import jax.numpy as jnp
from jax import lax
from jax.sharding import PartitionSpec as P

highest_score = lax.Precision.HIGHEST


def prefix(shard, axis, join, neutral, backward):
    count = lax.axis_size(axis)
    place = lax.axis_index(axis)
    ahead = count - 1 - place if backward else place
    gathered = jax.tree.map(
        lambda a, kind: lax.all_gather(a.astype(kind), axis), shard, (jnp.bfloat16, jnp.bfloat16)
    )
    state = jax.tree.map(lambda a, e: jnp.zeros_like(a) + jnp.asarray(e, a.dtype), shard, neutral)

    def one(hop, state):
        source = count - 1 - hop if backward else hop
        return join(
            state,
            jax.tree.map(
                lambda a, own: lax.dynamic_index_in_dim(a, source, 0, False).astype(own.dtype),
                gathered,
                shard,
            ),
        )

    return lax.fori_loop(0, ahead, one, state)


def block_decays(decay_rows):
    cum = jnp.cumsum(decay_rows, axis=-1)
    last = cum[:, -1]
    token_offset = jnp.arange(decay_rows.shape[-1])
    causal = token_offset[:, None] >= token_offset[None, :]
    gaps = jnp.where(causal[None], cum[:, :, None] - cum[:, None, :], -jnp.inf)
    return (cum, last, jnp.exp(gaps))


def silu_grad(upper):
    sigma = jax.nn.sigmoid(upper)
    return sigma * (1.0 + upper * (1.0 - sigma))


def split_heads(matrix, head_count):
    tokens_here = matrix.shape[0]
    return matrix.astype(jnp.float32).reshape(tokens_here, head_count, -1).transpose(1, 0, 2)


def join_heads(blocks):
    return blocks.transpose(1, 0, 2).reshape(blocks.shape[1], -1).astype(jnp.bfloat16)


def local(
    resid,
    queries,
    keys,
    values,
    log_decay,
    w_out,
    w_up,
    w_down,
    expert_ids,
    route_weights,
    cotangent,
):
    head_count = log_decay.shape[0]
    tokens_here = queries.shape[0]
    query_heads = split_heads(queries, head_count)
    head_keys = split_heads(keys, head_count)
    head_values = split_heads(values, head_count)
    cum, last, decay_matrix = block_decays(log_decay)
    keep_mask = jnp.exp(last[:, None] - cum)[..., None]
    router_scores = (
        jnp.einsum("htd,hid->hti", query_heads, head_keys, precision=highest_score) * decay_matrix
    )
    local_state = jnp.einsum(
        "hid,hie->hde", head_keys * keep_mask, head_values, precision=highest_score
    )

    def link(early, later):
        return (early[0] + later[0], jnp.exp(later[0])[:, None, None] * early[1] + later[1])

    blank = (jnp.zeros_like(last), jnp.zeros_like(local_state))
    _, incoming = prefix((last, local_state), "ctx", link, blank, False)
    inner = jnp.einsum("hti,hid->htd", router_scores, head_values, precision=highest_score)
    outer = jnp.exp(cum)[..., None] * jnp.einsum(
        "htd,hde->hte", query_heads, incoming, precision=highest_score
    )
    attn_heads = join_heads(inner + outer)
    width = w_out.shape[1]
    share = width // lax.axis_size("exp")
    columns = w_out
    attn = (
        lax.psum_scatter(
            lax.dot_general(
                columns, attn_heads, (((0,), (1,)), ((), ())), preferred_element_type=jnp.float32
            ).astype(jnp.bfloat16),
            "exp",
            scatter_dimension=0,
            tiled=True,
        )
        .astype(jnp.float32)
        .T.astype(jnp.bfloat16)
    )
    residual = (resid.astype(jnp.float32) + attn.astype(jnp.float32)).astype(jnp.bfloat16)
    residual_f = residual.astype(jnp.float32)
    square_sum = lax.psum(jnp.sum(residual_f * residual_f, axis=1), "exp")
    rstd = lax.rsqrt(square_sum / width + 1e-06)
    normed = (residual_f * rstd[:, None]).astype(jnp.bfloat16)
    expert_count = w_up.shape[0] * lax.axis_size("exp")
    capacity = 4 * tokens_here // expert_count
    onehot = (expert_ids[:, :, None] == jnp.arange(expert_count)[None, None, :]).astype(jnp.int32)
    flat = onehot.reshape(tokens_here * 2, expert_count)
    before = jnp.cumsum(flat, axis=0) - flat
    slots = jnp.sum(before * flat, axis=1).reshape(tokens_here, 2)
    position = expert_ids * capacity + slots
    place = position[:, :, None] == jnp.arange(expert_count * capacity)[None, None, :]
    picks = place.astype(jnp.bfloat16)
    placed = jnp.sum(place.astype(jnp.int32), axis=1).astype(jnp.bfloat16)
    sent_rows = lax.dot_general(
        placed, normed, (((0,), (0,)), ((), ())), preferred_element_type=jnp.float32
    )
    sent_rows = sent_rows.astype(jnp.bfloat16).reshape(expert_count, capacity, share)
    expert_in = lax.all_to_all(sent_rows, "exp", split_axis=0, concat_axis=2, tiled=True)
    all_rows = lax.all_gather(expert_in, "ctx", axis=1, tiled=True)
    upper = jnp.einsum("erd,edf->erf", all_rows, w_up, preferred_element_type=jnp.float32)
    act = jax.nn.silu(upper).astype(jnp.bfloat16)
    partial_out = jnp.einsum("erf,efd->erd", act, w_down, preferred_element_type=jnp.float32)
    expert_out = lax.psum_scatter(
        partial_out.astype(jnp.bfloat16), "ctx", scatter_dimension=1, tiled=True
    )
    returned = lax.all_to_all(expert_out, "exp", split_axis=2, concat_axis=0, tiled=True).reshape(
        expert_count * capacity, share
    )
    routed = jnp.einsum("tks,sd->tkd", picks, returned, preferred_element_type=jnp.float32)
    layer_out = (residual_f + jnp.sum(route_weights[:, :, None] * routed, axis=1)).astype(
        jnp.bfloat16
    )
    cot_f = cotangent.astype(jnp.float32)
    slot_weight = jnp.einsum(
        "tks,tk->s", place.astype(jnp.float32), route_weights, precision=highest_score
    )
    grad_rows_local = lax.dot_general(
        placed, cotangent, (((0,), (0,)), ((), ())), preferred_element_type=jnp.float32
    )
    grad_send = (
        (grad_rows_local * slot_weight[:, None])
        .astype(jnp.bfloat16)
        .reshape(expert_count, capacity, share)
    )
    grad_in = lax.all_to_all(grad_send, "exp", split_axis=0, concat_axis=2, tiled=True)
    grad_all = lax.all_gather(grad_in, "ctx", axis=1, tiled=True)
    grad_act = jnp.einsum("erd,efd->erf", grad_all, w_down, preferred_element_type=jnp.float32)
    grad_up = (grad_act * silu_grad(upper)).astype(jnp.bfloat16)
    partial_grad = jnp.einsum("erf,edf->erd", grad_up, w_up, preferred_element_type=jnp.float32)
    grad_expert = lax.psum_scatter(
        partial_grad.astype(jnp.bfloat16), "ctx", scatter_dimension=1, tiled=True
    )
    grad_back = lax.all_to_all(grad_expert, "exp", split_axis=2, concat_axis=0, tiled=True).reshape(
        expert_count * capacity, share
    )
    grad_normed = jnp.dot(placed, grad_back, preferred_element_type=jnp.float32)
    inner_dot = lax.psum(jnp.sum(grad_normed * residual_f, axis=1), "exp")
    grad_resid = (
        rstd[:, None] * grad_normed - residual_f * (rstd * rstd * rstd * inner_dot / width)[:, None]
    )
    resid_grad = (cot_f + grad_resid).astype(jnp.bfloat16)
    columns = w_out
    grad_flat = lax.dot_general(
        lax.all_gather(resid_grad, "exp", axis=1, tiled=True),
        columns,
        (((1,), (1,)), ((), ())),
        preferred_element_type=jnp.float32,
    )
    head_gradient = split_heads(grad_flat, head_count)
    local_grad = jnp.einsum(
        "hta,htb->hab",
        query_heads * jnp.exp(cum)[..., None],
        head_gradient,
        precision=highest_score,
    )

    def back_link(early, later):
        return (early[0] + later[0], later[1] + jnp.exp(later[0])[:, None, None] * early[1])

    blank_grad = (jnp.zeros_like(last), jnp.zeros_like(local_grad))
    _, carried_state = prefix((last, local_grad), "ctx", back_link, blank_grad, True)
    score_gradient = (
        jnp.einsum("coy,cwy->cow", head_gradient, head_values, precision=highest_score)
        * decay_matrix
    )
    query_grad = jnp.einsum("hti,hia->hta", score_gradient, head_keys, precision=highest_score)
    query_grad = query_grad + jnp.exp(cum)[..., None] * jnp.einsum(
        "htb,hab->hta", head_gradient, incoming, precision=highest_score
    )
    key_gradient = jnp.einsum("hti,hta->hia", score_gradient, query_heads, precision=highest_score)
    key_gradient = key_gradient + keep_mask * jnp.einsum(
        "qsv,qnv->qsn", head_values, carried_state, precision=highest_score
    )
    value_gradient = jnp.einsum(
        "nyw,nyx->nwx", router_scores, head_gradient, precision=highest_score
    )
    value_gradient = value_gradient + keep_mask * jnp.einsum(
        "sfc,scl->sfl", head_keys, carried_state, precision=highest_score
    )
    return (
        layer_out,
        resid_grad,
        join_heads(query_grad),
        join_heads(key_gradient),
        join_heads(value_gradient),
    )


def solution(mesh):
    return jax.shard_map(
        local,
        mesh=mesh,
        in_specs=(
            P("ctx", "exp"),
            P("ctx", "exp"),
            P("ctx", "exp"),
            P("ctx", "exp"),
            P("exp", "ctx"),
            P("exp", None),
            P("exp", None, "ctx"),
            P("exp", "ctx", None),
            P("ctx", None),
            P("ctx", None),
            P("ctx", "exp"),
        ),
        out_specs=(
            P("ctx", "exp"),
            P("ctx", "exp"),
            P("ctx", "exp"),
            P("ctx", "exp"),
            P("ctx", "exp"),
        ),
        check_vma=False,
    )
```

profile of v0, /device:TPU:32, one launch (start us, length us, event | category | flops | bytes accessed | tf_op | source)
XLA Modules:
  0.0 780.2 jit_solution(4295536002061562439)
XLA Ops:
  13.5 26.2 %all-gather = bf16[2048,128]{1,0:T(8,128)(2,1)} all-gather(bf16[128,128]{1,0:T(8,128)(2,1)S(1)} %convolution_convert_fusion.5), channel_id=2, replica_groups=mesh['ctx'=16,'exp'=32] {'ctx'}, dimensions={0}, use_global_device_ids=true | all-gather | bytes 557056 | tf_op jit(solution)/shard_map/all_gather | solution.py:14
  39.7 38.1 %all-reduce = bf16[16]{0:T(256)(128)(2,1)S(1)} all-reduce(bf16[16]{0:T(256)(128)(2,1)S(1)} %dynamic-update-slice), channel_id=1, replica_groups=mesh['ctx'=16,'exp'=32] {'ctx'}, use_global_device_ids=true, to_apply=%add | all-reduce | flops 16 | bytes 64
  84.2 131.8 %reduce-scatter.10.cloned.1.call-done = bf16[96,128]{1,0:T(8,128)(2,1)} async-done(((bf16[3072,128]{1,0:T(8,128)(2,1)}), bf16[96,128]{1,0:T(8,128)(2,1)}) %reduce-scatter.10.cloned.1.call-update) | async-done | bytes 24592 | tf_op jit(solution)/shard_map/reduce_scatter | solution.py:96
  216.8 45.9 %psum.14 = f32[128]{0:T(128)S(1)} all-reduce(f32[128]{0:T(128)S(1)} %get-tuple-element.215), channel_id=1, replica_groups=mesh['ctx'=16,'exp'=32] {'exp'}, use_global_device_ids=true, to_apply=%region_9.10 | all-reduce | flops 128 | bytes 1024 | tf_op jit(solution)/shard_map/psum | solution.py:109
  263.1 30.3 %all_to_all.66 = bf16[32,16,96]{2,1,0:T(8,128)(2,1)S(1)} all-to-all(bf16[32,16,96]{2,1,0:T(8,128)(2,1)S(1)} %bitcast.175), channel_id=1, replica_groups=mesh['ctx'=16,'exp'=32] {'exp'}, dimensions={0} | all-to-all | bytes 196608 | tf_op jit(solution)/shard_map/all_to_all | solution.py:126
  295.0 20.5 %all_to_all.67 = bf16[32,16,96]{2,1,0:T(8,128)(2,1)S(1)} all-to-all(bf16[32,16,96]{2,1,0:T(8,128)(2,1)S(1)} %bitcast.176), channel_id=1, replica_groups=mesh['ctx'=16,'exp'=32] {'exp'}, dimensions={0} | all-to-all | bytes 196608 | tf_op jit(solution)/shard_map/all_to_all | solution.py:153
  316.4 29.6 %all-gather.5.cloned.1.call-done = bf16[1,256,3072]{2,1,0:T(8,128)(2,1)} async-done(((bf16[1,16,3072]{2,1,0:T(8,128)(2,1)}), bf16[1,256,3072]{2,1,0:T(8,128)(2,1)}) %all-gather.5.cloned.1.call-update) | async-done | bytes 1572880 | tf_op jit(solution)/shard_map/all_gather | solution.py:127
  349.1 59.1 %all-gather.7.cloned.1.call-done = bf16[1,256,3072]{2,1,0:T(8,128)(2,1)} async-done(((bf16[1,16,3072]{2,1,0:T(8,128)(2,1)}), bf16[1,256,3072]{2,1,0:T(8,128)(2,1)}) %all-gather.7.cloned.1.call-update) | async-done | bytes 1572880 | tf_op jit(solution)/shard_map/all_gather | solution.py:154
  408.2 5.2 fusion.1
  415.9 86.2 %reduce-scatter.8.cloned.1.call-done = bf16[1,16,3072]{2,1,0:T(8,128)(2,1)} async-done(((bf16[1,256,3072]{2,1,0:T(8,128)(2,1)}), bf16[1,16,3072]{2,1,0:T(8,128)(2,1)}) %reduce-scatter.8.cloned.1.call-update) | async-done | bytes 98320 | tf_op jit(solution)/shard_map/reduce_scatter | solution.py:158
  502.1 3.6 copy.109
  506.2 18.0 %reduce.2 = bf16[3072,16]{1,0:T(8,128)(2,1)S(1)} reduce(bf16[3072,1,16]{2,1,0:T(2,128)(2,1)} %bitcast.168, bf16[]{:T(256)} %broadcast.70), dimensions={1}, to_apply=%bitcast.130.reduce_sub_computation | reduce | bytes 196610
  525.5 12.9 %all-to-all-start.3 = ((bf16[32,2,768]{2,1,0:T(2,128)(2,1)}), bf16[32,2,768]{2,1,0:T(2,128)(2,1)}, u32[]{:S(2)}, u32[]{:S(2)}) async-start(bf16[32,2,768]{2,1,0:T(2,128)(2,1)} %reshape.274), calls=%async_computation.5 | async-start | bytes 196608 | tf_op jit(solution)/shard_map/all_to_all | solution.py:161
  538.3 56.6 %reduce-scatter.6.cloned.1.call-done = bf16[1,16,3072]{2,1,0:T(8,128)(2,1)} async-done(((bf16[1,256,3072]{2,1,0:T(8,128)(2,1)}), bf16[1,16,3072]{2,1,0:T(8,128)(2,1)}) %reduce-scatter.6.cloned.1.call-update) | async-done | bytes 98320 | tf_op jit(solution)/shard_map/reduce_scatter | solution.py:131
  595.0 3.6 copy.103
  598.6 18.0 %reduce.3 = bf16[3072,16]{1,0:T(8,128)(2,1)S(1)} reduce(bf16[3072,1,16]{2,1,0:T(2,128)(2,1)} %bitcast.169, bf16[]{:T(256)} %broadcast.70), dimensions={1}, to_apply=%bitcast.128.reduce_sub_computation | reduce | bytes 196610
  617.9 12.8 %all-to-all-start.1 = ((bf16[32,2,768]{2,1,0:T(2,128)(2,1)}), bf16[32,2,768]{2,1,0:T(2,128)(2,1)S(1)}, u32[]{:S(2)}, u32[]{:S(2)}) async-start(bf16[32,2,768]{2,1,0:T(2,128)(2,1)} %reshape.272), calls=%async_computation.2 | async-start | bytes 196608 | tf_op jit(solution)/shard_map/all_to_all | solution.py:134
  630.7 4.9 reshape.275
  635.6 3.3 copy.110
  639.4 45.4 %psum.15 = f32[128]{0:T(128)S(1)} all-reduce(f32[128]{0:T(128)S(1)} %get-tuple-element.221), channel_id=1, replica_groups=mesh['ctx'=16,'exp'=32] {'exp'}, use_global_device_ids=true, to_apply=%region_14.15 | all-reduce | flops 128 | bytes 1024 | tf_op jit(solution)/shard_map/psum | solution.py:165
  687.8 3.4 copy.104
  693.9 33.0 %all_gather.32 = bf16[128,3072]{0,1:T(8,128)(2,1)S(1)} all-gather(bf16[128,96]{0,1:T(8,128)(2,1)S(1)} %get-tuple-element.217), channel_id=1, replica_groups=mesh['ctx'=16,'exp'=32] {'exp'}, dimensions={1}, use_global_device_ids=true | all-gather | bytes 811008 | tf_op jit(solution)/shard_map/all_gather | solution.py:172
  728.6 23.3 %all-gather.1 = bf16[2048,128]{1,0:T(8,128)(2,1)S(1)} all-gather(bf16[128,128]{1,0:T(8,128)(2,1)S(1)} %convolution_convert_fusion.4), channel_id=3, replica_groups=mesh['ctx'=16,'exp'=32] {'ctx'}, dimensions={0}, use_global_device_ids=true | all-gather | bytes 557056 | tf_op jit(solution)/shard_map/all_gather | solution.py:14
  751.9 19.2 %while.27 = (s32[]{:T(128)}, f32[1,128,128]{2,1,0:T(8,128)S(1)}, s32[]{:T(128)}, bf16[16,1,128,128]{3,2,1,0:T(8,128)(2,1)S(1)}, bf16[16,1]{0,1:T(2,128)(2,1)S(1)...) while((s32[]{:T(128)}, f32[1,128,128]{2,1,0:T(8,128)S(1)}, s32[]{:T(128)}, ...), condition=%wide.region_16.17_spmd, body=%wide.region_15.16_spmd.sunk | while | flops 49158 | bytes 163997 | solution.py:29
  (154 shorter events, 52.9 us)
Async XLA Ops:
  7.2 401.1 %copy-start = (bf16[1,384,3072]{2,1,0:T(8,128)(2,1)S(1)}, bf16[1,384,3072]{2,1,0:T(8,128)(2,1)}, u32[]{:S(2)}) copy-start(bf16[1,384,3072]{2,1,0:T(8,128)(2,1)} %param.22) | copy-start | bytes 7077892
  7.2 70.7 %copy-start.5 = (bf16[128,128]{1,0:T(8,128)(2,1)S(1)}, bf16[128,128]{1,0:T(8,128)(2,1)}, u32[]{:S(2)}) copy-start(bf16[128,128]{1,0:T(8,128)(2,1)} %param.17) | copy-start | bytes 98308
  7.2 70.9 %copy-start.3 = (bf16[128,128]{1,0:T(8,128)(2,1)S(1)}, bf16[128,128]{1,0:T(8,128)(2,1)}, u32[]{:S(2)}) copy-start(bf16[128,128]{1,0:T(8,128)(2,1)} %param.18) | copy-start | bytes 98308
  7.2 70.7 %copy-start.7 = (bf16[128,128]{1,0:T(8,128)(2,1)S(1)}, bf16[128,128]{1,0:T(8,128)(2,1)}, u32[]{:S(2)}) copy-start(bf16[128,128]{1,0:T(8,128)(2,1)} %param.16) | copy-start | bytes 98308
  7.2 71.6 %copy-start.1 = (bf16[128,3072]{1,0:T(8,128)(2,1)S(1)}, bf16[128,3072]{1,0:T(8,128)(2,1)}, u32[]{:S(2)}) copy-start(bf16[128,3072]{1,0:T(8,128)(2,1)} %param.20) | copy-start | bytes 2359300
  7.2 208.8 %reduce-scatter.10.cloned.1.call-start = ((), (), s32[]{:S(2)}) async-start(), calls=%async_computation.11 | async-start | bytes 811008 | tf_op jit(solution)/shard_map/reduce_scatter | solution.py:96
  8.4 71.8 %copy-start.18 = (f32[1,128]{1,0:T(1,128)}, f32[1,128]{1,0:T(1,128)S(1)}, u32[]{:S(2)}) copy-start(f32[1,128]{1,0:T(1,128)S(1)} %reduce_window_sum.26) | copy-start | bytes 1540
  10.3 67.5 %copy-start.16 = (f32[128]{0:T(128)}, f32[128]{0:T(128)S(1)}, u32[]{:S(2)}) copy-start(f32[128]{0:T(128)S(1)} %get-tuple-element.220) | copy-start | bytes 1540
  10.3 69.8 %copy-start.14 = (f32[128]{0:T(128)}, f32[128]{0:T(128)S(1)}, u32[]{:S(2)}) copy-start(f32[128]{0:T(128)S(1)} %get-tuple-element.219) | copy-start | bytes 1540
  80.1 135.9 %copy-start.13 = (bf16[128,96]{0,1:T(8,128)(2,1)S(1)}, bf16[128,96]{0,1:T(8,128)(2,1)}, u32[]{:S(2)}) copy-start(bf16[128,96]{0,1:T(8,128)(2,1)} %param.15) | copy-start | bytes 73732
  82.5 211.9 %copy-start.22 = (f32[128,2]{0,1:T(2,128)S(1)}, f32[128,2]{0,1:T(2,128)}, u32[]{:S(2)}) copy-start(f32[128,2]{0,1:T(2,128)} %param.24) | copy-start | bytes 3076
  82.5 212.2 %copy-start.12 = (bf16[128,96]{0,1:T(8,128)(2,1)S(1)}, bf16[128,96]{0,1:T(8,128)(2,1)}, u32[]{:S(2)}) copy-start(bf16[128,96]{0,1:T(8,128)(2,1)} %param.25) | copy-start | bytes 73732
  82.5 263.5 %all-gather.5.cloned.1.call-start = ((), (), s32[]{:S(2)}) async-start(), calls=%async_computation.7 | async-start | bytes 1671168 | tf_op jit(solution)/shard_map/all_gather | solution.py:127
  294.3 113.9 %all-gather.7.cloned.1.call-start = ((), (), s32[]{:S(2)}) async-start(), calls=%async_computation.9 | async-start | bytes 1671168 | tf_op jit(solution)/shard_map/all_gather | solution.py:154
  316.4 185.7 %reduce-scatter.8.cloned.1.call-start = ((), (), s32[]{:S(2)}) async-start(), calls=%async_computation.10 | async-start | bytes 1671168 | tf_op jit(solution)/shard_map/reduce_scatter | solution.py:158
  413.5 181.5 %reduce-scatter.6.cloned.1.call-start = ((), (), s32[]{:S(2)}) async-start(), calls=%async_computation.8 | async-start | bytes 1671168 | tf_op jit(solution)/shard_map/reduce_scatter | solution.py:131
  525.5 92.4 %all-to-all-start.3 = ((bf16[32,2,768]{2,1,0:T(2,128)(2,1)}), bf16[32,2,768]{2,1,0:T(2,128)(2,1)}, u32[]{:S(2)}, u32[]{:S(2)}) async-start(bf16[32,2,768]{2,1,0:T(2,128)(2,1)} %reshape.274), calls=%async_computation.5 | async-start | bytes 196608 | tf_op jit(solution)/shard_map/all_to_all | solution.py:161
  617.9 67.5 %all-to-all-start.1 = ((bf16[32,2,768]{2,1,0:T(2,128)(2,1)}), bf16[32,2,768]{2,1,0:T(2,128)(2,1)S(1)}, u32[]{:S(2)}, u32[]{:S(2)}) async-start(bf16[32,2,768]{2,1,0:T(2,128)(2,1)} %reshape.272), calls=%async_computation.2 | async-start | bytes 196608 | tf_op jit(solution)/shard_map/all_to_all | solution.py:134
  687.7 39.1 %copy-start.2 = (bf16[128,3072]{1,0:T(8,128)(2,1)S(1)}, bf16[128,3072]{1,0:T(8,128)(2,1)}, u32[]{:S(2)}) copy-start(bf16[128,3072]{1,0:T(8,128)(2,1)} %param.20) | copy-start | bytes 2359300
  691.3 35.9 %copy-start.8 = (bf16[128,128]{1,0:T(8,128)(2,1)S(1)}, bf16[128,128]{1,0:T(8,128)(2,1)}, u32[]{:S(2)}) copy-start(bf16[128,128]{1,0:T(8,128)(2,1)} %param.16) | copy-start | bytes 98308
  691.4 36.2 %copy-start.10 = (f32[128,128]{1,0:T(8,128)S(1)}, f32[128,128]{1,0:T(8,128)}, u32[]{:S(2)}) copy-start(f32[128,128]{1,0:T(8,128)} %copy-done.9) | copy-start | bytes 196612
  691.4 36.5 %copy-start.4 = (bf16[128,128]{1,0:T(8,128)(2,1)S(1)}, bf16[128,128]{1,0:T(8,128)(2,1)}, u32[]{:S(2)}) copy-start(bf16[128,128]{1,0:T(8,128)(2,1)} %param.18) | copy-start | bytes 98308
  691.4 36.5 %copy-start.19 = (f32[1,128]{1,0:T(1,128)S(1)}, f32[1,128]{1,0:T(1,128)}, u32[]{:S(2)}) copy-start(f32[1,128]{1,0:T(1,128)} %copy-done.18) | copy-start | bytes 1540
  727.3 43.9 %copy-start.17 = (f32[128]{0:T(128)S(1)}, f32[128]{0:T(128)}, u32[]{:S(2)}) copy-start(f32[128]{0:T(128)} %copy-done.16) | copy-start | bytes 1540
  (8 other events, 169.5 us)
Sparse Core Ops, SparseCore 0:
  82.6 133.4 reduce-scatter.9
  294.4 51.4 all-gather.4
  349.5 58.7 all-gather.6
  413.6 88.4 reduce-scatter.7
  506.6 88.3 reduce-scatter.5
where the time goes:
time: 783 us; the launch traced here: 780 us
  waiting for transfers between devices  363 us (46%)
  blocking collectives  263 us (34%)
  other arithmetic  51.2 us (7%)
  local copies, waits for them, and re-layouts  41.8 us (5%)
  starting transfers between devices  26.1 us (3%)
  matrix products  19.5 us (2%)
  between operations  15 us (2%)
    reduce_scatter x1, waiting for transfers between devices, local(): lax.psum_scatter(lax.dot_general(columns, attn_heads, (((0,), (1,)), ((),...  132 us
    reduce_scatter x1, waiting for transfers between devices, local(): lax.psum_scatter(partial_grad.astype(jnp.bfloat16), 'ctx', scatter_dimens...  86.2 us
    all_gather x1, waiting for transfers between devices, local(): grad_all = lax.all_gather(grad_in, 'ctx', axis=1, tiled=True)  59.1 us
    reduce_scatter x1, waiting for transfers between devices, local(): lax.psum_scatter(partial_out.astype(jnp.bfloat16), 'ctx', scatter_dimensi...  56.6 us
    all_gather x2, blocking collectives, prefix(): lax.all_gather(a.astype(kind), axis)  49.5 us
    psum x1, blocking collectives, local(): square_sum = lax.psum(jnp.sum(residual_f * residual_f, axis=1), 'exp')  45.9 us
    psum x1, blocking collectives, local(): inner_dot = lax.psum(jnp.sum(grad_normed * residual_f, axis=1), 'exp')  45.4 us
    unnamed x1, blocking collectives  38.1 us
  transfers between devices with their start and end apart: 7, of which 5 were waited for; matrix products, arithmetic and copies ran while one was open for 8% of the time, Pallas kernels for 0%

commit v1 on v0

v1 whole, which is shorter than its diff:
```python
import jax
import jax.numpy as jnp
from jax import lax
from jax.sharding import PartitionSpec as P

highest = lax.Precision.HIGHEST
bf16 = jnp.bfloat16
f32 = jnp.float32


def mm(a, b, dims):
    return lax.dot_general(a, b, (dims, ((), ())), preferred_element_type=f32)


def mm_high(a, b, dims):
    return lax.dot_general(a, b, (dims, ((), ())), precision=highest, preferred_element_type=f32)


def gather_ctx(block):
    count = lax.axis_size("ctx")
    copies = jnp.broadcast_to(block[None], (count, *block.shape))
    return lax.all_to_all(copies, "ctx", 0, 0)


def between(lasts, low, high):
    count = lasts.shape[0]
    block = jnp.arange(count)
    inside = (block[None, :] > low) & (block[None, :] < high)
    return jnp.exp(jnp.sum(jnp.where(inside, lasts[None, :], 0.0), axis=1))


def local(
    resid, queries, keys, values, log_decay, w_out, w_up, w_down, expert_ids, route_weights, cotangent
):
    n_ctx, n_exp = lax.axis_size("ctx"), lax.axis_size("exp")
    chips = n_exp // 2
    me_ctx, me_exp = lax.axis_index("ctx"), lax.axis_index("exp")
    core = lax.rem(me_exp, 2)
    tokens, dh = queries.shape
    width = w_out.shape[1]
    share = width // n_exp
    cap = 4 * tokens // n_exp
    partner = [(i, i ^ 1) for i in range(n_exp)]
    same_core = [[2 * z + c for z in range(chips)] for c in range(2)]

    q, k, v = queries.astype(f32), keys.astype(f32), values.astype(f32)
    at = jnp.arange(tokens)
    causal = at[:, None] >= at[None, :]
    cum = jnp.sum(jnp.where(causal, log_decay, 0.0), axis=1)
    last = cum[-1]
    decay = jnp.exp(jnp.where(causal, cum[:, None] - cum[None, :], -jnp.inf))
    grow = jnp.exp(cum)[:, None]
    keep = jnp.exp(last - cum)[:, None]
    scores = mm_high(q, k, ((1,), (1,))) * decay
    state = mm_high(k * keep, v, ((0,), (0,)))
    high = lax.reduce_precision(last, 8, 7)
    mid = lax.reduce_precision(last - high, 8, 7)
    low = last - high - mid
    row = jnp.arange(16)[:, None]
    tail = jnp.where(row == 0, high, jnp.where(row == 1, mid, jnp.where(row == 2, low, 0.0)))
    packed = jnp.concatenate([state, jnp.broadcast_to(tail, (16, dh))], axis=0).astype(bf16)
    arrived = gather_ctx(packed).astype(f32)
    lasts = jnp.sum(arrived[:, dh : dh + 3, 0], axis=1)
    blocks = jnp.arange(n_ctx)
    weight_in = jnp.where(blocks < me_ctx, between(lasts, blocks[:, None], me_ctx), 0.0)
    incoming = jnp.sum(weight_in[:, None, None] * arrived[:, :dh], axis=0)
    attn_heads = (
        mm_high(scores, v, ((1,), (0,))) + grow * mm_high(q, incoming, ((1,), (0,)))
    ).astype(bf16)

    w_parts = w_out.T.reshape(chips, 2, share, dh).transpose(1, 0, 2, 3)
    partial = mm(w_parts.reshape(width, dh), attn_heads, ((1,), (1,))).astype(bf16)
    partial = partial.reshape(2, chips, share, tokens)
    mine = lax.dynamic_index_in_dim(partial, core, 0, False)
    other = lax.dynamic_index_in_dim(partial, 1 - core, 0, False)
    other = lax.ppermute(other, "exp", partner)
    pair = (mine.astype(f32) + other.astype(f32)).astype(bf16)
    pieces = lax.all_to_all(pair, "exp", 0, 0, axis_index_groups=same_core)
    attn = jnp.sum(pieces.astype(f32), axis=0).T.astype(bf16)
    residual = (resid.astype(f32) + attn.astype(f32)).astype(bf16)

    chosen = (expert_ids[:, :, None] == jnp.arange(n_exp)[None, None, :]).astype(f32)
    earlier = (at[:, None] > at[None, :]).astype(bf16)
    before = mm(earlier, jnp.sum(chosen, axis=1).astype(bf16), ((1,), (0,)))
    slots = jnp.sum(before[:, None, :] * chosen, axis=2).astype(jnp.int32)
    position = expert_ids * cap + slots
    picks = jnp.concatenate(
        [
            (position[:, j][:, None] == jnp.arange(n_exp * cap)[None, :]).astype(bf16)
            for j in range(2)
        ],
        axis=0,
    )
    cot = cotangent.astype(f32)
    parts = jnp.concatenate(
        [
            jnp.concatenate([residual, (route_weights[:, j : j + 1] * cot).astype(bf16)], axis=1)
            for j in range(2)
        ],
        axis=0,
    )
    sent = mm(picks, parts, ((0,), (0,))).astype(bf16).reshape(n_exp, cap, 2 * share)
    rows = lax.all_to_all(sent, "exp", 0, 0)
    rows = rows.reshape(n_exp, cap, 2, share).transpose(2, 1, 0, 3).reshape(2, cap, width)
    rows_f = rows[0].astype(f32)
    rstd = lax.rsqrt(jnp.mean(rows_f * rows_f, axis=1, keepdims=True) + 1e-6)
    normed = (rows_f * rstd).astype(bf16)

    everyone = gather_ctx(jnp.concatenate([normed, rows[1]], axis=0))
    x = everyone[:, :cap].reshape(n_ctx * cap, width)
    g = everyone[:, cap:].reshape(n_ctx * cap, width)
    up_w, down_w = w_up[0], w_down[0]
    upper = mm(x, up_w, ((1,), (0,)))
    grad_act = mm(g, down_w, ((1,), (1,)))
    sigma = jax.nn.sigmoid(upper)
    act = (upper * sigma).astype(bf16)
    grad_up = (grad_act * (sigma * (1.0 + upper * (1.0 - sigma)))).astype(bf16)
    out = mm(act, down_w, ((1,), (0,))).astype(bf16).reshape(n_ctx, cap, width)
    back = mm(grad_up, up_w, ((1,), (1,))).astype(bf16).reshape(n_ctx, cap, width)
    sums = lax.all_to_all(jnp.concatenate([out, back], axis=1), "ctx", 0, 0)
    sums = jnp.sum(sums.astype(f32), axis=0)
    grad_rows = sums[cap:]
    inner = jnp.sum(grad_rows * rows_f, axis=1, keepdims=True)
    grad_rows = rstd * grad_rows - rows_f * (rstd * rstd * rstd * inner / width)
    both = jnp.stack([sums[:cap], grad_rows]).astype(bf16)
    both = both.reshape(2, cap, n_exp, share).transpose(2, 1, 0, 3).reshape(n_exp, cap, 2 * share)
    returned = lax.all_to_all(both, "exp", 0, 0).reshape(n_exp * cap, 2 * share)
    routed = mm(picks, returned, ((1,), (0,)))
    first, second = routed[:tokens], routed[tokens:]
    layer_out = (
        residual.astype(f32)
        + (route_weights[:, :1] * first[:, :share] + route_weights[:, 1:] * second[:, :share])
    ).astype(bf16)
    resid_grad = (cot + (first[:, share:] + second[:, share:])).astype(bf16)

    own_parts = lax.all_gather(resid_grad.T, "exp", axis_index_groups=same_core)
    own_parts = own_parts.reshape(chips * share, tokens)
    other_parts = lax.ppermute(own_parts, "exp", partner)
    w_halves = w_parts.reshape(2, chips * share, dh)
    w_mine = lax.dynamic_index_in_dim(w_halves, core, 0, False)
    w_other = lax.dynamic_index_in_dim(w_halves, 1 - core, 0, False)
    grad_heads = mm(own_parts, w_mine, ((0,), (0,))) + mm(other_parts, w_other, ((0,), (0,)))
    state_grad = mm_high(q * grow, grad_heads, ((0,), (0,)))
    arrived = gather_ctx(state_grad.astype(bf16)).astype(f32)
    weight_back = jnp.where(blocks > me_ctx, between(lasts, me_ctx, blocks[:, None]), 0.0)
    carried = jnp.sum(weight_back[:, None, None] * arrived, axis=0)
    score_grad = mm_high(grad_heads, v, ((1,), (1,))) * decay
    q_grad = mm_high(score_grad, k, ((1,), (0,)))
    q_grad = q_grad + grow * mm_high(grad_heads, incoming, ((1,), (1,)))
    k_grad = mm_high(score_grad, q, ((0,), (0,)))
    k_grad = k_grad + keep * mm_high(v, carried, ((1,), (1,)))
    v_grad = mm_high(scores, grad_heads, ((0,), (0,)))
    v_grad = v_grad + keep * mm_high(k, carried, ((1,), (0,)))
    return (layer_out, resid_grad, q_grad.astype(bf16), k_grad.astype(bf16), v_grad.astype(bf16))


def solution(mesh):
    both = P("ctx", "exp")
    rows = P("ctx", None)
    return jax.shard_map(
        local,
        mesh=mesh,
        in_specs=(
            both, both, both, both, P("exp", "ctx"), P("exp", None),
            P("exp", None, "ctx"), P("exp", "ctx", None), rows, rows, both,
        ),
        out_specs=(both,) * 5,
        check_vma=False,
    )
```

time: 783 us -> 304 us (0.39)
  waiting for transfers between devices: 363 us -> 40.9 us
  blocking collectives: 263 us -> 171 us
  other arithmetic: 51.2 us -> 17.5 us
  local copies, waits for them, and re-layouts: 41.8 us -> 20.1 us
  between operations: 15 us -> 4.78 us
    reduce_scatter x3 -> x0, waiting for transfers between devices: 275 us -> none  [the longest x1 132 us: local(): lax.psum_scatter(lax.dot_general(columns, attn_heads, (((0,), (1,)), ((),...]
    psum x2 -> x0, blocking collectives: 91.3 us -> none  [the longest x1 45.9 us: local(): square_sum = lax.psum(jnp.sum(residual_f * residual_f, axis=1), 'exp')]
    all_to_all x2 -> x4, blocking collectives: 50.8 us -> 141 us  [the longest x1 42.6 us: gather_ctx(): return lax.all_to_all(copies, 'ctx', 0, 0)]
    all_gather x2 -> x0, waiting for transfers between devices: 88.7 us -> none  [the longest x1 59.1 us: local(): grad_all = lax.all_gather(grad_in, 'ctx', axis=1, tiled=True)]
    all_gather x3 -> x1, blocking collectives: 82.5 us -> 30.2 us  [local(): own_parts = lax.all_gather(resid_grad.T, 'exp', axis_index_groups=same_core)]
    all_to_all x2 -> x3, waiting for transfers between devices: 0.01 us -> 38.3 us  [the longest x2 19.2 us: gather_ctx(): return lax.all_to_all(copies, 'ctx', 0, 0)]
    unnamed x1 -> x0, blocking collectives: 38.1 us -> none
    unnamed x2 -> x0, other arithmetic: 36 us -> none
  transfers between devices with their start and end apart: 7 -> 5, of which waited for: 5 -> 5; matrix products, arithmetic and copies ran while one was open for 8% -> 3% of each run, Pallas kernels for 0% -> 0%
where the time goes in v1:
time: 304 us; the launch traced here: 303 us
  blocking collectives  171 us (56%)
  waiting for transfers between devices  40.9 us (13%)
  starting transfers between devices  29.8 us (10%)
  local copies, waits for them, and re-layouts  20.1 us (7%)
  matrix products  18.8 us (6%)
  other arithmetic  17.5 us (6%)
  between operations  4.78 us (2%)
    all_to_all x1, blocking collectives, gather_ctx(): return lax.all_to_all(copies, 'ctx', 0, 0)  42.6 us
    all_to_all x1, blocking collectives, local(): sums = lax.all_to_all(jnp.concatenate([out, back], axis=1), 'ctx', 0, 0)  41.8 us
    all_gather x1, blocking collectives, local(): own_parts = lax.all_gather(resid_grad.T, 'exp', axis_index_groups=same_core)  30.2 us
    all_to_all x1, blocking collectives, local(): rows = lax.all_to_all(sent, 'exp', 0, 0)  28.9 us
    all_to_all x1, blocking collectives, local(): returned = lax.all_to_all(both, 'exp', 0, 0).reshape(n_exp * cap, 2 * share)  27.4 us
    all_to_all x2, waiting for transfers between devices, gather_ctx(): return lax.all_to_all(copies, 'ctx', 0, 0)  19.2 us
    all_to_all x1, waiting for transfers between devices, local(): pieces = lax.all_to_all(pair, 'exp', 0, 0, axis_index_groups=same_core)  19 us
    all_to_all x1, starting transfers between devices, local(): pieces = lax.all_to_all(pair, 'exp', 0, 0, axis_index_groups=same_core)  15.2 us
  transfers between devices with their start and end apart: 5, of which 5 were waited for; matrix products, arithmetic and copies ran while one was open for 3% of the time, Pallas kernels for 0%

profile of v1, /device:TPU:32, one launch (start us, length us, event | category | flops | bytes accessed | tf_op | source)
XLA Modules:
  0.0 302.8 jit_solution(17839427135067348058)
XLA Ops:
  9.9 7.2 %all-to-all-start = ((bf16[16,144,128]{2,1,0:T(8,128)(2,1)}), bf16[16,144,128]{2,1,0:T(8,128)(2,1)}, u32[]{:S(2)}, u32[]{:S(2)}) async-start(bf16[16,144,128]{2,1,0:T(8,128)(2,1)} %broadcast_in_dim.66), calls=%async_computation | async-start | bytes 1179648 | tf_op jit(solution)/shard_map/all_to_all | solution.py:22
  20.5 8.6 %all-to-all-done = bf16[16,144,128]{2,1,0:T(8,128)(2,1)} async-done(((bf16[16,144,128]{2,1,0:T(8,128)(2,1)}), bf16[16,144,128]{2,1,0:T(8,128)(2,1)}, u32[]{:S(2)}, u32[]{:S(2)}) %all-to-all-start) | async-done | bytes 589856 | tf_op jit(solution)/shard_map/all_to_all | solution.py:22
  33.3 2.3 copy.36
  35.6 1.8 dynamic-slice_bitcast_fusion
  37.4 1.9 collective-permute-start
  39.3 1.9 collective-permute-done
  41.2 1.9 fusion.27
  43.0 15.2 %all-to-all-start.1 = ((bf16[16,96,128]{2,1,0:T(8,128)(2,1)}), bf16[16,96,128]{2,1,0:T(8,128)(2,1)S(1)}, u32[]{:S(2)}, u32[]{:S(2)}) async-start(bf16[16,96,128]{2,1,0:T(8,128)(2,1)} %fusion.27), calls=%async_computation.1 | async-start | bytes 786432 | tf_op jit(solution)/shard_map/all_to_all | solution.py:78
  59.2 1.4 fusion.52
  61.4 19.0 %all-to-all-done.1 = bf16[16,96,128]{2,1,0:T(8,128)(2,1)S(1)} async-done(((bf16[16,96,128]{2,1,0:T(8,128)(2,1)}), bf16[16,96,128]{2,1,0:T(8,128)(2,1)S(1)}, u32[]{:S(2)}, u32[]{:S(2)}) %all-to-all-start.1) | async-done | bytes 393248 | tf_op jit(solution)/shard_map/all_to_all | solution.py:78
  82.5 1.8 convolution_convert_fusion.3
  85.3 28.9 %all_to_all.35 = bf16[32,16,192]{2,1,0:T(8,128)(2,1)} all-to-all(bf16[32,16,192]{2,1,0:T(8,128)(2,1)S(1)} %bitcast.127), channel_id=1, replica_groups=mesh['ctx'=16,'exp'=32] {'exp'}, dimensions={0} | all-to-all | bytes 393216 | tf_op jit(solution)/shard_map/all_to_all | solution.py:103
  118.2 42.6 %all_to_all.36 = bf16[16,32,3072]{2,1,0:T(8,128)(2,1)S(1)} all-to-all(bf16[16,32,3072]{2,1,0:T(8,128)(2,1)S(1)} %broadcast_in_dim.110), channel_id=1, replica_groups=mesh['ctx'=16,'exp'=32] {'ctx'}, dimensions={0} | all-to-all | bytes 6291456 | tf_op jit(solution)/shard_map/all_to_all | solution.py:22
  160.8 1.5 fusion.74
  164.8 2.2 convolution_convert_fusion.1
  167.0 5.3 %convolution_convert_fusion = bf16[256,3072]{1,0:T(8,128)(2,1)} fusion(bf16[1,3072,384]{2,1,0:T(8,128)(2,1)} %param.17, bf16[256,3072]{1,0:T(8,128)(2,1)} %bitcast.123, bf16[1,384,3072]{2,1,0:T(8,128)(2,1)S(1)} %copy-done, f32[256,384]{1,0:T(8,128)} %copy-done.22), kind=kOutput, calls=%fused_computation.1 | convolution fusion | flops 1209630720 | bytes 8257536 | tf_op jit(solution)/shard_map/dot_general | solution.py:12
  172.4 2.2 pad_maximum_fusion
  174.5 41.8 %all_to_all.37 = bf16[16,32,3072]{2,1,0:T(8,128)(2,1)S(1)} all-to-all(bf16[16,32,3072]{2,1,0:T(8,128)(2,1)S(1)} %pad_maximum_fusion), channel_id=1, replica_groups=mesh['ctx'=16,'exp'=32] {'ctx'}, dimensions={0} | all-to-all | bytes 6291456 | tf_op jit(solution)/shard_map/all_to_all | solution.py:120
  219.5 27.4 %all_to_all.38 = bf16[32,16,192]{2,1,0:T(8,128)(2,1)S(1)} all-to-all(bf16[32,16,192]{2,1,0:T(8,128)(2,1)} %reshape.171), channel_id=1, replica_groups=mesh['ctx'=16,'exp'=32] {'exp'}, dimensions={0} | all-to-all | bytes 393216 | tf_op jit(solution)/shard_map/all_to_all | solution.py:127
  248.1 1.4 fusion.54
  249.5 30.2 %all-gather = bf16[1536,128]{1,0:T(8,128)(2,1)S(1)} all-gather(bf16[96,128]{1,0:T(8,128)(2,1)S(1)} %bitcast.129), channel_id=2, replica_groups={{0,2,4,6,8,10,12,14,16,18,20,22,24,26,28,30},{1,3,5,7,9,11,13,15,17,19,..., dimensions={0}, use_global_device_ids=true | all-gather | bytes 417792 | tf_op jit(solution)/shard_map/all_gather | solution.py:136
  279.7 1.9 collective-permute-start.1
  285.4 3.6 %all-to-all-start.6 = ((bf16[16,128,128]{2,1,0:T(8,128)(2,1)}), bf16[16,128,128]{2,1,0:T(8,128)(2,1)S(1)}, u32[]{:S(2)}, u32[]{:S(2)}) async-start(bf16[16,128,128]{2,1,0:T(8,128)(2,1)} %broadcast_in_dim.111), calls=%async_computation.6 | async-start | bytes 1048576 | tf_op jit(solution)/shard_map/all_to_all | solution.py:22
  290.3 10.6 %all-to-all-done.6 = bf16[16,128,128]{2,1,0:T(8,128)(2,1)S(1)} async-done(((bf16[16,128,128]{2,1,0:T(8,128)(2,1)}), bf16[16,128,128]{2,1,0:T(8,128)(2,1)S(1)}, u32[]{:S(2)}, u32[]{:S(2)}) %all-to-all-start.6) | async-done | bytes 524320 | tf_op jit(solution)/shard_map/all_to_all | solution.py:22
  (113 shorter events, 35.4 us)
Async XLA Ops:
  0.6 164.2 %copy-start = (bf16[1,384,3072]{2,1,0:T(8,128)(2,1)S(1)}, bf16[1,384,3072]{2,1,0:T(8,128)(2,1)}, u32[]{:S(2)}) copy-start(bf16[1,384,3072]{2,1,0:T(8,128)(2,1)} %param.18) | copy-start | bytes 7077892
  0.6 16.5 %copy-start.1 = (bf16[128,3072]{1,0:T(8,128)(2,1)S(1)}, bf16[128,3072]{1,0:T(8,128)(2,1)}, u32[]{:S(2)}) copy-start(bf16[128,3072]{1,0:T(8,128)(2,1)} %param.16) | copy-start | bytes 2359300
  9.0 10.6 %copy-start.6 = (bf16[128,128]{1,0:T(8,128)(2,1)S(1)}, bf16[128,128]{1,0:T(8,128)(2,1)}, u32[]{:S(2)}) copy-start(bf16[128,128]{1,0:T(8,128)(2,1)} %param.13) | copy-start | bytes 98308
  9.0 10.5 %copy-start.8 = (bf16[128,128]{1,0:T(8,128)(2,1)S(1)}, bf16[128,128]{1,0:T(8,128)(2,1)}, u32[]{:S(2)}) copy-start(bf16[128,128]{1,0:T(8,128)(2,1)} %param.12) | copy-start | bytes 98308
  9.9 10.4 %copy-start.4 = (bf16[128,128]{1,0:T(8,128)(2,1)S(1)}, bf16[128,128]{1,0:T(8,128)(2,1)}, u32[]{:S(2)}) copy-start(bf16[128,128]{1,0:T(8,128)(2,1)} %param.14) | copy-start | bytes 98308
  9.9 19.2 %all-to-all-start = ((bf16[16,144,128]{2,1,0:T(8,128)(2,1)}), bf16[16,144,128]{2,1,0:T(8,128)(2,1)}, u32[]{:S(2)}, u32[]{:S(2)}) async-start(bf16[16,144,128]{2,1,0:T(8,128)(2,1)} %broadcast_in_dim.66), calls=%async_computation | async-start | bytes 1179648 | tf_op jit(solution)/shard_map/all_to_all | solution.py:22
  33.3 25.0 %copy-start.15 = (s32[128,2]{0,1:T(2,128)S(1)}, s32[128,2]{0,1:T(2,128)}, u32[]{:S(2)}) copy-start(s32[128,2]{0,1:T(2,128)} %param.19) | copy-start | bytes 3076
  37.4 3.8 %collective-permute-start = (bf16[16,96,128]{2,1,0:T(8,128)(2,1)}, bf16[16,96,128]{2,1,0:T(8,128)(2,1)S(1)}, u32[]{:S(2)}, u32[]{:S(2)}) collective-permute-start(bf16[16,96,128]{2,1,0:T(8,128)(2,1)} %dynamic-slice_bitcast_fusion), channel_id=1, source_target_pairs={{0,1},{1,0},{2,3},{3,2},{4,5},{5,4},{6,7},{7,6},{8,9},{9,8},{10,11... | collective-permute-start | bytes 1179656 | tf_op jit(solution)/shard_map/ppermute | solution.py:76
  43.0 37.4 %all-to-all-start.1 = ((bf16[16,96,128]{2,1,0:T(8,128)(2,1)}), bf16[16,96,128]{2,1,0:T(8,128)(2,1)S(1)}, u32[]{:S(2)}, u32[]{:S(2)}) async-start(bf16[16,96,128]{2,1,0:T(8,128)(2,1)} %fusion.27), calls=%async_computation.1 | async-start | bytes 786432 | tf_op jit(solution)/shard_map/all_to_all | solution.py:78
  59.2 1.4 copy-start.16
  59.2 1.4 copy-start.18
  116.4 1.8 copy-start.19
  160.8 2.2 copy-start.21
  164.1 0.8 copy-start.22
  216.8 31.2 %copy-start.17 = (f32[128]{0:T(128)S(1)}, f32[128]{0:T(128)}, u32[]{:S(2)}) copy-start(f32[128]{0:T(128)} %copy-done.16) | copy-start | bytes 1540
  217.5 29.5 %copy-start.14 = (pred[128,512]{1,0:T(32,128)(4,1)S(1)}, pred[128,512]{1,0:T(32,128)(4,1)}, u32[]{:S(2)}) copy-start(pred[128,512]{1,0:T(32,128)(4,1)} %get-tuple-element.21) | copy-start | bytes 196612
  217.9 65.7 %copy-start.9 = (bf16[128,128]{1,0:T(8,128)(2,1)S(1)}, bf16[128,128]{1,0:T(8,128)(2,1)}, u32[]{:S(2)}) copy-start(bf16[128,128]{1,0:T(8,128)(2,1)} %param.12) | copy-start | bytes 98308
  217.9 66.1 %copy-start.5 = (bf16[128,128]{1,0:T(8,128)(2,1)S(1)}, bf16[128,128]{1,0:T(8,128)(2,1)}, u32[]{:S(2)}) copy-start(bf16[128,128]{1,0:T(8,128)(2,1)} %param.14) | copy-start | bytes 98308
  248.1 40.9 %copy-start.7 = (bf16[128,128]{1,0:T(8,128)(2,1)S(1)}, bf16[128,128]{1,0:T(8,128)(2,1)}, u32[]{:S(2)}) copy-start(bf16[128,128]{1,0:T(8,128)(2,1)} %param.13) | copy-start | bytes 98308
  248.1 41.0 %copy-start.11 = (f32[128,128]{1,0:T(8,128)S(1)}, f32[128,128]{1,0:T(8,128)}, u32[]{:S(2)}) copy-start(f32[128,128]{1,0:T(8,128)} %copy-done.10) | copy-start | bytes 196612
  249.5 40.8 %copy-start.12 = (bf16[128,96]{0,1:T(8,128)(2,1)}, bf16[128,96]{0,1:T(8,128)(2,1)S(1)}, u32[]{:S(2)}) copy-start(bf16[128,96]{0,1:T(8,128)(2,1)S(1)} %get-tuple-element.11) | copy-start | bytes 73732
  249.5 39.9 %copy-start.3 = (f32[128,128]{1,0:T(8,128)S(1)}, f32[128,128]{1,0:T(8,128)}, u32[]{:S(2)}) copy-start(f32[128,128]{1,0:T(8,128)} %copy-done.2) | copy-start | bytes 196612
  279.7 3.6 %collective-permute-start.1 = (bf16[1536,128]{1,0:T(8,128)(2,1)S(1)}, bf16[1536,128]{1,0:T(8,128)(2,1)S(1)}, u32[]{:S(2)}, u32[]{:S(2)}) collective-permute-start(bf16[1536,128]{1,0:T(8,128)(2,1)S(1)} %all-gather), channel_id=1, source_target_pairs={{0,1},{1,0},{2,3},{3,2},{4,5},{5,4},{6,7},{7,6},{8,9},{9,8},{10,11... | collective-permute-start | bytes 1179656 | tf_op jit(solution)/shard_map/ppermute | solution.py:138
  285.4 15.6 %all-to-all-start.6 = ((bf16[16,128,128]{2,1,0:T(8,128)(2,1)}), bf16[16,128,128]{2,1,0:T(8,128)(2,1)S(1)}, u32[]{:S(2)}, u32[]{:S(2)}) async-start(bf16[16,128,128]{2,1,0:T(8,128)(2,1)} %broadcast_in_dim.111), calls=%async_computation.6 | async-start | bytes 1048576 | tf_op jit(solution)/shard_map/all_to_all | solution.py:22
  (4 other events, 2.6 us)

commit v2 on v1

v2 whole, which is shorter than its diff:
```python
import functools

import jax
import jax.numpy as jnp
from jax import lax
from jax.experimental import pallas as pl
from jax.experimental.pallas import tpu as pltpu
from jax.sharding import PartitionSpec as P

bf16 = jnp.bfloat16
f32 = jnp.float32
ROWS = 16


def mm(a, b, dims):
    return lax.dot_general(a, b, (dims, ((), ())), preferred_element_type=f32)


def mm_high(a, b, dims):
    return lax.dot_general(
        a, b, (dims, ((), ())), precision=lax.Precision.HIGHEST, preferred_element_type=f32
    )


def iota(shape, axis):
    return lax.broadcasted_iota(jnp.int32, shape, axis)


def turned(column):
    n = column.shape[0]
    return jnp.sum(jnp.where(iota((n, n), 0) == iota((n, n), 1), column, 0.0), axis=0, keepdims=True)


def run_kernel(body, outs, args, smem=0, flops=0, moved=0, limit=24):
    vmem = pl.BlockSpec(memory_space=pltpu.VMEM)
    specs = [pl.BlockSpec(memory_space=pltpu.SMEM)] * smem + [vmem] * (len(args) - smem)
    return pl.pallas_call(
        body,
        out_shape=[jax.ShapeDtypeStruct(shape, dtype) for shape, dtype in outs],
        in_specs=specs,
        out_specs=[vmem] * len(outs),
        compiler_params=pltpu.CompilerParams(vmem_limit_bytes=limit << 20),
        cost_estimate=pl.CostEstimate(flops=flops, bytes_accessed=moved, transcendentals=0),
    )(*args)


def running(decay_row):
    n = decay_row.shape[1]
    causal = iota((n, n), 0) >= iota((n, n), 1)
    return jnp.sum(jnp.where(causal, decay_row, 0.0), axis=1, keepdims=True)


def state_kernel(keys, values, log_decay, packed):
    cum = running(log_decay[...])
    n = cum.shape[0]
    last = cum[n - 1 :, :]
    kept = keys[...].astype(f32) * jnp.exp(last - cum)
    state = mm_high(kept, values[...].astype(f32), ((0,), (0,))).astype(bf16)
    dh = state.shape[1]
    high = last.astype(bf16).astype(f32)
    mid = (last - high).astype(bf16).astype(f32)
    low = last - high - mid
    row = iota((ROWS, dh), 0)
    tail = jnp.where(row == 0, high, jnp.where(row == 1, mid, jnp.where(row == 2, low, 0.0)))
    for block in range(packed.shape[0]):
        packed[block, :dh, :] = state
        packed[block, dh:, :] = tail.astype(bf16)


def inner_kernel(queries, keys, values, log_decay, w_out, scores, inner, decay, grow, keep, w_turned):
    cum = running(log_decay[...])
    n = cum.shape[0]
    causal = iota((n, n), 0) >= iota((n, n), 1)
    gaps = jnp.where(causal, cum - turned(cum), 0.0)
    fall = jnp.where(causal, jnp.exp(gaps), 0.0)
    pairs = mm_high(queries[...].astype(f32), keys[...].astype(f32), ((1,), (1,))) * fall
    scores[...] = pairs
    decay[...] = fall
    inner[...] = mm_high(pairs, values[...].astype(f32), ((1,), (0,)))
    grow[...] = jnp.broadcast_to(jnp.exp(cum), grow.shape)
    keep[...] = jnp.broadcast_to(jnp.exp(cum[n - 1 :, :] - cum), keep.shape)
    dh = w_out.shape[0]
    for start in range(0, w_out.shape[1], dh):
        w_turned[start : start + dh, :] = w_out[:, start : start + dh].astype(f32).T.astype(bf16)


def route_kernel(ids, weights, cotangent, picks, picks_turned, cot_parts, *, cap):
    tokens = ids.shape[0]
    slots_all = picks.shape[1]
    experts = slots_all // cap
    chosen = [(ids[:, j : j + 1] == iota((tokens, experts), 1)).astype(f32) for j in range(2)]
    earlier = (iota((tokens, tokens), 0) > iota((tokens, tokens), 1)).astype(f32).astype(bf16)
    before = mm(earlier, (chosen[0] + chosen[1]).astype(bf16), ((1,), (0,)))
    cot = cotangent[...].astype(f32)
    for j in range(2):
        slot = jnp.sum(before * chosen[j], axis=1, keepdims=True)
        position = ids[:, j : j + 1].astype(f32) * cap + slot
        at = slice(j * tokens, (j + 1) * tokens)
        along = iota((tokens, slots_all), 1).astype(f32)
        picks[at, :] = (position == along).astype(f32).astype(bf16)
        down = iota((slots_all, tokens), 0).astype(f32)
        picks_turned[:, at] = (turned(position) == down).astype(f32).astype(bf16)
        cot_parts[at, :] = (weights[:, j : j + 1] * cot).astype(bf16)


def heads_kernel(place, arrived, queries, inner, grow, w_turned, mine, other, incoming):
    me, core = place[0], place[1]
    blocks = arrived.shape[0]
    dh = queries.shape[1]
    total = jnp.zeros((dh, dh), f32)
    gap = jnp.zeros((1, dh), f32)
    for block in reversed(range(blocks)):
        weight = jnp.where(block < me, jnp.exp(gap), 0.0)
        total = total + weight * arrived[block, :dh, :].astype(f32)
        last = jnp.sum(arrived[block, dh:, :].astype(f32), axis=0, keepdims=True)
        gap = gap + jnp.where(block < me, last, 0.0)
    incoming[...] = total
    outer = mm_high(queries[...].astype(f32), total, ((1,), (0,)))
    heads = (inner[...] + grow[...] * outer).astype(bf16)
    chips, share, _ = mine.shape
    turned_heads = heads.astype(f32).T.astype(bf16)
    for chip in range(chips):
        start = 2 * chip * share
        both = mm(w_turned[start : start + 2 * share, :], turned_heads, ((1,), (0,))).astype(bf16)
        even, odd = both[:share], both[share:]

        @pl.when(core == 0)
        def _():
            mine[chip] = even
            other[chip] = odd

        @pl.when(core != 0)
        def _():
            mine[chip] = odd
            other[chip] = even


def send_kernel(pieces, resid, cot_parts, picks_turned, residual, sent):
    attn = jnp.sum(pieces[...].astype(f32), axis=0).T.astype(bf16).astype(f32)
    total = (resid[...].astype(f32) + attn).astype(bf16)
    residual[...] = total
    tokens = total.shape[0]
    experts, cap, _ = sent.shape
    share = total.shape[1]
    placed = picks_turned[...]
    rows = mm(placed[:, :tokens] + placed[:, tokens:], total, ((1,), (0,))).astype(bf16)
    grads = mm(placed, cot_parts[...], ((1,), (0,))).astype(bf16)
    sent[:, :, :share] = rows.reshape(experts, cap, share)
    sent[:, :, share : 2 * share] = grads.reshape(experts, cap, share)


def norm_kernel(rows, packed, own, rstd_out):
    experts, cap, _ = rows.shape
    share = packed.shape[2] // experts
    whole = jnp.concatenate([rows[e, :, :share].astype(f32) for e in range(experts)], axis=1)
    grads = jnp.concatenate(
        [rows[e, :, share : 2 * share].astype(f32) for e in range(experts)], axis=1
    ).astype(bf16)
    width = whole.shape[1]
    rstd = lax.rsqrt(jnp.sum(whole * whole, axis=1, keepdims=True) / width + 1e-6)
    own[...] = whole.astype(bf16)
    rstd_out[...] = jnp.broadcast_to(rstd, rstd_out.shape)
    normed = (whole * rstd).astype(bf16)
    for block in range(packed.shape[0]):
        packed[block, :cap, :] = normed
        packed[block, cap:, :] = grads


def expert_kernel(everyone, w_up, w_down, sums, *, step):
    blocks, both, width = everyone.shape
    cap = both // 2
    rows = blocks * cap
    hidden = w_up.shape[1]

    def forward(i, carry):
        upper, grad_act = carry
        at = pl.ds(pl.multiple_of(i * step, step), step)
        x = everyone[:, :cap, at].reshape(rows, step)
        g = everyone[:, cap:, at].reshape(rows, step)
        upper = upper + mm(x, w_up[at, :], ((1,), (0,)))
        grad_act = grad_act + mm(g, w_down[:, at], ((1,), (1,)))
        return upper, grad_act

    zero = jnp.zeros((rows, hidden), f32)
    upper, grad_act = lax.fori_loop(0, width // step, forward, (zero, zero))
    sigma = 1.0 / (1.0 + jnp.exp(-upper))
    act = (upper * sigma).astype(bf16)
    grad_up = (grad_act * (sigma * (1.0 + upper * (1.0 - sigma)))).astype(bf16)

    def backward(i, carry):
        at = pl.ds(pl.multiple_of(i * step, step), step)
        out = mm(act, w_down[:, at], ((1,), (0,))).astype(bf16)
        back = mm(grad_up, w_up[at, :], ((1,), (1,))).astype(bf16)
        sums[:, :cap, at] = out.reshape(blocks, cap, step)
        sums[:, cap:, at] = back.reshape(blocks, cap, step)
        return carry

    lax.fori_loop(0, width // step, backward, 0)


def back_kernel(sums, own, rstd_in, returned):
    experts, cap, _ = returned.shape
    total = jnp.sum(sums[...].astype(f32), axis=0)
    out, grads = total[:cap], total[cap:]
    width = out.shape[1]
    share = width // experts
    rows = own[...].astype(f32)
    rstd = rstd_in[:, :1]
    grads = grads.astype(bf16).astype(f32)
    inner = jnp.sum(grads * rows, axis=1, keepdims=True)
    grads = rstd * grads - rows * (rstd * rstd * rstd * inner / width)
    for e in range(experts):
        at = slice(e * share, (e + 1) * share)
        returned[e, :, :share] = out[:, at].astype(bf16)
        returned[e, :, share : 2 * share] = grads[:, at].astype(bf16)


def join_kernel(returned, picks, weights, residual, cotangent, layer_out, resid_grad, turned_grad):
    tokens, share = residual.shape
    slots_all = picks.shape[1]
    rows = returned[...].reshape(slots_all, returned.shape[2])
    first = mm(picks[:tokens, :], rows, ((1,), (0,)))
    second = mm(picks[tokens:, :], rows, ((1,), (0,)))
    routed = weights[:, :1] * first[:, :share] + weights[:, 1:] * second[:, :share]
    layer_out[...] = (residual[...].astype(f32) + routed).astype(bf16)
    summed = first[:, share : 2 * share] + second[:, share : 2 * share]
    grad = (cotangent[...].astype(f32) + summed).astype(bf16)
    resid_grad[...] = grad
    turned_grad[...] = grad.astype(f32).T.astype(bf16)


def state_grad_kernel(turned_grads, w_out, queries, grow, grad_heads, packed):
    flipped = mm(w_out[...], turned_grads[...], ((1,), (0,)))
    grads = flipped.T
    grad_heads[...] = grads
    state = mm_high(queries[...].astype(f32) * grow[...], grads, ((0,), (0,))).astype(bf16)
    for block in range(packed.shape[0]):
        packed[block] = state


def grads_kernel(
    grad_heads, queries, keys, values, scores, decay, grow, incoming, q_grad, k_part, v_part
):
    grads = grad_heads[...]
    score_grad = mm_high(grads, values[...].astype(f32), ((1,), (1,))) * decay[...]
    direct = mm_high(score_grad, keys[...].astype(f32), ((1,), (0,)))
    carried = mm_high(grads, incoming[...], ((1,), (1,)))
    q_grad[...] = (direct + grow[...] * carried).astype(bf16)
    k_part[...] = mm_high(score_grad, queries[...].astype(f32), ((0,), (0,)))
    v_part[...] = mm_high(scores[...], grads, ((0,), (0,)))


def last_kernel(place, arrived, tails, keys, values, keep, k_part, v_part, k_grad, v_grad):
    me = place[0]
    blocks, dh, _ = arrived.shape
    total = jnp.zeros((dh, dh), f32)
    gap = jnp.zeros((1, dh), f32)
    for block in range(blocks):
        weight = jnp.where(block > me, jnp.exp(gap), 0.0)
        total = total + weight * arrived[block].astype(f32)
        last = jnp.sum(tails[block, dh:, :].astype(f32), axis=0, keepdims=True)
        gap = gap + jnp.where(block > me, last, 0.0)
    from_values = mm_high(values[...].astype(f32), total, ((1,), (1,)))
    from_keys = mm_high(keys[...].astype(f32), total, ((1,), (0,)))
    k_grad[...] = (k_part[...] + keep[...] * from_values).astype(bf16)
    v_grad[...] = (v_part[...] + keep[...] * from_keys).astype(bf16)


def local(
    resid, queries, keys, values, log_decay, w_out, w_up, w_down, expert_ids, route_weights, cotangent
):
    n_ctx, n_exp = lax.axis_size("ctx"), lax.axis_size("exp")
    chips = n_exp // 2
    place = jnp.stack([lax.axis_index("ctx"), lax.rem(lax.axis_index("exp"), 2)]).astype(jnp.int32)
    tokens, dh = queries.shape
    width = w_out.shape[1]
    share = width // n_exp
    cap = 4 * tokens // n_exp
    partner = [(i, i ^ 1) for i in range(n_exp)]
    same_core = [[2 * z + c for z in range(chips)] for c in range(2)]
    square = (tokens, dh)
    small = dict(flops=10_000_000, moved=1_000_000)

    [packed] = run_kernel(
        state_kernel, [((n_ctx, dh + ROWS, dh), bf16)], (keys, values, log_decay), **small
    )
    arrived = lax.all_to_all(packed, "ctx", 0, 0)
    scores, inner, decay, grow, keep, w_turned = run_kernel(
        inner_kernel,
        [((tokens, tokens), f32), (square, f32), ((tokens, tokens), f32), (square, f32), (square, f32)]
        + [((width, dh), bf16)],
        (queries, keys, values, log_decay, w_out),
        **small,
    )
    picks, picks_turned, cot_parts = run_kernel(
        functools.partial(route_kernel, cap=cap),
        [((2 * tokens, n_exp * cap), bf16), ((n_exp * cap, 2 * tokens), bf16)]
        + [((2 * tokens, share), bf16)],
        (expert_ids, route_weights, cotangent),
        **small,
    )
    mine, other, incoming = run_kernel(
        heads_kernel,
        [((chips, share, tokens), bf16)] * 2 + [((dh, dh), f32)],
        (place, arrived, queries, inner, grow, w_turned),
        smem=1,
        **small,
    )
    other = lax.ppermute(other, "exp", partner)
    pair = (mine.astype(f32) + other.astype(f32)).astype(bf16)
    pieces = lax.all_to_all(pair, "exp", 0, 0, axis_index_groups=same_core)
    residual, sent = run_kernel(
        send_kernel,
        [((tokens, share), bf16), ((n_exp, cap, 2 * share), bf16)],
        (pieces, resid, cot_parts, picks_turned),
        **small,
    )
    rows = lax.all_to_all(sent, "exp", 0, 0)
    packed, own, rstd = run_kernel(
        norm_kernel,
        [((n_ctx, 2 * cap, width), bf16), ((cap, width), bf16), ((cap, 128), f32)],
        (rows,),
        **small,
    )
    everyone = lax.all_to_all(packed, "ctx", 0, 0)
    [sums] = run_kernel(
        functools.partial(expert_kernel, step=256),
        [((n_ctx, 2 * cap, width), bf16)],
        (everyone, w_up[0], w_down[0]),
        flops=2_400_000_000,
        moved=11_000_000,
    )
    sums = lax.all_to_all(sums, "ctx", 0, 0)
    [returned] = run_kernel(
        back_kernel, [((n_exp, cap, 2 * share), bf16)], (sums, own, rstd), **small
    )
    returned = lax.all_to_all(returned, "exp", 0, 0)
    layer_out, resid_grad, turned_grad = run_kernel(
        join_kernel,
        [((tokens, share), bf16), ((tokens, share), bf16), ((share, tokens), bf16)],
        (returned, picks, route_weights, residual, cotangent),
        **small,
    )
    turned_grads = lax.all_gather(turned_grad, "exp", tiled=True)
    grad_heads, packed = run_kernel(
        state_grad_kernel,
        [(square, f32), ((n_ctx, dh, dh), bf16)],
        (turned_grads, w_out, queries, grow),
        **small,
    )
    states = lax.all_to_all(packed, "ctx", 0, 0)
    q_grad, k_part, v_part = run_kernel(
        grads_kernel,
        [(square, bf16), (square, f32), (square, f32)],
        (grad_heads, queries, keys, values, scores, decay, grow, incoming),
        **small,
    )
    k_grad, v_grad = run_kernel(
        last_kernel,
        [(square, bf16), (square, bf16)],
        (place, states, arrived, keys, values, keep, k_part, v_part),
        smem=1,
        **small,
    )
    return layer_out, resid_grad, q_grad, k_grad, v_grad


def solution(mesh):
    both = P("ctx", "exp")
    rows = P("ctx", None)
    return jax.shard_map(
        local,
        mesh=mesh,
        in_specs=(
            both, both, both, both, P("exp", "ctx"), P("exp", None),
            P("exp", None, "ctx"), P("exp", "ctx", None), rows, rows, both,
        ),
        out_specs=(both,) * 5,
        check_vma=False,
    )
```

time: 304 us -> 271 us (0.89)
  Pallas kernels: 0 us -> 20.3 us
  matrix products: 18.8 us -> 0 us
  other arithmetic: 17.5 us -> 0.92 us
  local copies, waits for them, and re-layouts: 20.1 us -> 8.89 us
  between operations: 4.78 us -> 0.82 us
    pallas_call x0 -> x12, Pallas kernels: none -> 20.3 us  [run_kernel(): pl.pallas_call(body, out_shape=[jax.ShapeDtypeStruct(shape, dtype) for sh...]
    dot_general x21 -> x0, matrix products: 18.8 us -> none  [the longest x9 13.4 us: mm(): return lax.dot_general(a, b, (dims, ((), ())), preferred_element_type=f32)]
    convert_element_type x5 -> x0, other arithmetic: 4.79 us -> none  [the longest x1 1.44 us: local(): resid_grad = (cot + (first[:, share:] + second[:, share:])).astype(bf16)]
    convert_element_type x3 -> x0, local copies, waits for them, and re-layouts: 4.48 us -> none  [the longest x1 2.31 us: local(): mm(w_parts.reshape(width, dh), attn_heads, ((1,), (1,))).astype(bf16)]
    unnamed x47 -> x44, local copies, waits for them, and re-layouts: 4.59 us -> 8.89 us
    reduce_sum x11 -> x0, other arithmetic: 3.68 us -> none  [the longest x1 0.92 us: local(): cum = jnp.sum(jnp.where(causal, log_decay, 0.0), axis=1)]
  transfers between devices with their start and end apart: 5 -> 4, of which waited for: 5 -> 4; matrix products, arithmetic and copies ran while one was open for 3% -> 1% of each run, Pallas kernels for 0% -> 1%
where the time goes in v2:
time: 271 us; the launch traced here: 270 us
  blocking collectives  172 us (63%)
  waiting for transfers between devices  39.7 us (15%)
  starting transfers between devices  27.7 us (10%)
  Pallas kernels  20.3 us (7%)
  local copies, waits for them, and re-layouts  8.89 us (3%)
    all_to_all x1, blocking collectives, local(): everyone = lax.all_to_all(packed, 'ctx', 0, 0)  42.9 us
    all_to_all x1, blocking collectives, local(): sums = lax.all_to_all(sums, 'ctx', 0, 0)  41.8 us
    all_gather x1, blocking collectives, local(): turned_grads = lax.all_gather(turned_grad, 'exp', tiled=True)  30.9 us
    all_to_all x1, blocking collectives, local(): rows = lax.all_to_all(sent, 'exp', 0, 0)  28.8 us
    all_to_all x1, blocking collectives, local(): returned = lax.all_to_all(returned, 'exp', 0, 0)  27.2 us
    all_to_all x1, waiting for transfers between devices, local(): pieces = lax.all_to_all(pair, 'exp', 0, 0, axis_index_groups=same_core)  21.2 us
    pallas_call x12, Pallas kernels, run_kernel(): pl.pallas_call(body, out_shape=[jax.ShapeDtypeStruct(shape, dtype) for sh...  20.3 us
    all_to_all x1, starting transfers between devices, local(): pieces = lax.all_to_all(pair, 'exp', 0, 0, axis_index_groups=same_core)  15.2 us
  transfers between devices with their start and end apart: 4, of which 4 were waited for; matrix products, arithmetic and copies ran while one was open for 1% of the time, Pallas kernels for 1%

profile of v2, /device:TPU:32, one launch (start us, length us, event | category | flops | bytes accessed | tf_op | source)
XLA Modules:
  0.0 269.9 jit_solution(12521312878903634344)
XLA Ops:
  1.4 0.8 copy-done.10
  2.8 1.2 shard_map.146
  4.0 7.0 %all-to-all-start = ((bf16[16,144,128]{2,1,0:T(8,128)(2,1)}), bf16[16,144,128]{2,1,0:T(8,128)(2,1)S(1)}, u32[]{:S(2)}, u32[]{:S(2)}) async-start(bf16[16,144,128]{2,1,0:T(8,128)(2,1)} %shard_map.146), calls=%async_computation | async-start | bytes 1179648 | tf_op jit(solution)/shard_map/all_to_all | solution.py:287
  11.1 1.1 copy-done
  12.2 0.8 copy-done.4
  15.7 7.2 %all-to-all-done.arrived.tails = bf16[16,144,128]{2,1,0:T(8,128)(2,1)S(1)} async-done(((bf16[16,144,128]{2,1,0:T(8,128)(2,1)}), bf16[16,144,128]{2,1,0:T(8,128)(2,1)S(1)}, u32[]{:S(2)}, u32[]{:S(2)}) %all-to-all-start) | async-done | bytes 589856 | tf_op jit(solution)/shard_map/all_to_all | solution.py:287
  22.9 0.8 copy-done.5
  23.7 3.5 %shard_map.148 = (bf16[16,96,128]{2,1,0:T(8,128)(2,1)S(1)}, bf16[16,96,128]{2,1,0:T(8,128)(2,1)S(1)}, f32[128,128]{1,0:T(8,128)S(1)}) custom-call(s32[2]{0:T(128)S(1)} %pad_add_fusion.place, bf16[16,144,128]{2,1,0:T(8,128)(2,1)S(1)} %all-to-all-done.arrived.tails, bf16[128,128]{1,0:T(8,128)(2,1)S(1)} %copy-done.5, f32[128,128]{1,0:T(8,128)S(1)} %get-tuple-element.32.inner, ...), custom_call_target="tpu_custom_call" | custom-call | flops 10000000 | bytes 1000000 | tf_op jit(solution)/shard_map/pallas_call | solution.py:37
  27.2 1.9 collective-permute-start
  29.1 1.7 collective-permute-done
  30.8 0.8 add_convert_fusion
  31.6 15.2 %all-to-all-start.1 = ((bf16[16,96,128]{2,1,0:T(8,128)(2,1)}), bf16[16,96,128]{2,1,0:T(8,128)(2,1)S(1)}, u32[]{:S(2)}, u32[]{:S(2)}) async-start(bf16[16,96,128]{2,1,0:T(8,128)(2,1)} %add_convert_fusion), calls=%async_computation.1 | async-start | bytes 786432 | tf_op jit(solution)/shard_map/all_to_all | solution.py:311
  47.9 21.2 %all-to-all-done.1.pieces = bf16[16,96,128]{2,1,0:T(8,128)(2,1)S(1)} async-done(((bf16[16,96,128]{2,1,0:T(8,128)(2,1)}), bf16[16,96,128]{2,1,0:T(8,128)(2,1)S(1)}, u32[]{:S(2)}, u32[]{:S(2)}) %all-to-all-start.1) | async-done | bytes 393248 | tf_op jit(solution)/shard_map/all_to_all | solution.py:311
  69.5 28.8 %all_to_all.35.rows = bf16[32,16,192]{2,1,0:T(8,128)(2,1)S(1)} all-to-all(bf16[32,16,192]{2,1,0:T(8,128)(2,1)S(1)} %get-tuple-element.39), channel_id=1, replica_groups=mesh['ctx'=16,'exp'=32] {'exp'}, dimensions={0} | all-to-all | bytes 393216 | tf_op jit(solution)/shard_map/all_to_all | solution.py:318
  98.7 42.9 %all_to_all.36.everyone = bf16[16,32,3072]{2,1,0:T(8,128)(2,1)S(1)} all-to-all(bf16[16,32,3072]{2,1,0:T(8,128)(2,1)S(1)} %get-tuple-element.40), channel_id=1, replica_groups=mesh['ctx'=16,'exp'=32] {'ctx'}, dimensions={0} | all-to-all | bytes 6291456 | tf_op jit(solution)/shard_map/all_to_all | solution.py:325
  141.6 8.4 %shard_map.152 = bf16[16,32,3072]{2,1,0:T(8,128)(2,1)S(1)} custom-call(bf16[16,32,3072]{2,1,0:T(8,128)(2,1)S(1)} %all_to_all.36.everyone, bf16[3072,384]{1,0:T(8,128)(2,1)S(1)} %bitcast.4, bf16[384,3072]{1,0:T(8,128)(2,1)S(1)} %bitcast.5), custom_call_target="tpu_custom_call" | custom-call | flops 2400000000 | bytes 11000000 | tf_op jit(solution)/shard_map/pallas_call | solution.py:37
  149.9 41.8 %all_to_all.37.sums = bf16[16,32,3072]{2,1,0:T(8,128)(2,1)S(1)} all-to-all(bf16[16,32,3072]{2,1,0:T(8,128)(2,1)S(1)} %shard_map.152), channel_id=1, replica_groups=mesh['ctx'=16,'exp'=32] {'ctx'}, dimensions={0} | all-to-all | bytes 6291456 | tf_op jit(solution)/shard_map/all_to_all | solution.py:333
  192.4 27.2 %all_to_all.38.returned = bf16[32,16,192]{2,1,0:T(8,128)(2,1)S(1)} all-to-all(bf16[32,16,192]{2,1,0:T(8,128)(2,1)S(1)} %shard_map.153), channel_id=1, replica_groups=mesh['ctx'=16,'exp'=32] {'exp'}, dimensions={0} | all-to-all | bytes 393216 | tf_op jit(solution)/shard_map/all_to_all | solution.py:337
  220.0 30.9 %all_gather.3.turned_grads = bf16[3072,128]{1,0:T(8,128)(2,1)S(1)} all-gather(bf16[96,128]{1,0:T(8,128)(2,1)S(1)} %get-tuple-element.47), channel_id=1, replica_groups=mesh['ctx'=16,'exp'=32] {'exp'}, dimensions={0}, use_global_device_ids=true | all-gather | bytes 811008 | tf_op jit(solution)/shard_map/all_gather | solution.py:344
  251.0 1.5 shard_map.155
  252.5 3.6 %all-to-all-start.6 = ((bf16[16,128,128]{2,1,0:T(8,128)(2,1)}), bf16[16,128,128]{2,1,0:T(8,128)(2,1)S(1)}, u32[]{:S(2)}, u32[]{:S(2)}) async-start(bf16[16,128,128]{2,1,0:T(8,128)(2,1)} %get-tuple-element.53), calls=%async_computation.6 | async-start | bytes 1048576 | tf_op jit(solution)/shard_map/all_to_all | solution.py:351
  257.5 1.2 shard_map.156
  258.7 9.7 %all-to-all-done.6.arrived = bf16[16,128,128]{2,1,0:T(8,128)(2,1)S(1)} async-done(((bf16[16,128,128]{2,1,0:T(8,128)(2,1)}), bf16[16,128,128]{2,1,0:T(8,128)(2,1)S(1)}, u32[]{:S(2)}, u32[]{:S(2)}) %all-to-all-start.6) | async-done | bytes 524320 | tf_op jit(solution)/shard_map/all_to_all | solution.py:351
  268.3 1.6 shard_map.157
  (47 shorter events, 8.5 us)
Async XLA Ops:
  0.6 0.8 copy-start.7
  1.4 0.8 copy-start.10
  2.2 0.7 copy-start.13
  2.8 44.0 %copy-start.15 = (bf16[128,96]{0,1:T(8,128)(2,1)S(1)}, bf16[128,96]{0,1:T(8,128)(2,1)}, u32[]{:S(2)}) copy-start(bf16[128,96]{0,1:T(8,128)(2,1)} %param.21) | copy-start | bytes 73732
  2.8 44.2 %copy-start.16 = (bf16[128,96]{0,1:T(8,128)(2,1)S(1)}, bf16[128,96]{0,1:T(8,128)(2,1)}, u32[]{:S(2)}) copy-start(bf16[128,96]{0,1:T(8,128)(2,1)} %param.11) | copy-start | bytes 73732
  2.8 44.3 %copy-start.17 = (f32[128,2]{0,1:T(2,128)S(1)}, f32[128,2]{0,1:T(2,128)}, u32[]{:S(2)}) copy-start(f32[128,2]{0,1:T(2,128)} %param.20) | copy-start | bytes 3076
  2.8 44.4 %copy-start.18 = (s32[128,2]{0,1:T(2,128)S(1)}, s32[128,2]{0,1:T(2,128)}, u32[]{:S(2)}) copy-start(s32[128,2]{0,1:T(2,128)} %param.19) | copy-start | bytes 3076
  4.0 18.9 %all-to-all-start = ((bf16[16,144,128]{2,1,0:T(8,128)(2,1)}), bf16[16,144,128]{2,1,0:T(8,128)(2,1)S(1)}, u32[]{:S(2)}, u32[]{:S(2)}) async-start(bf16[16,144,128]{2,1,0:T(8,128)(2,1)} %shard_map.146), calls=%async_computation | async-start | bytes 1179648 | tf_op jit(solution)/shard_map/all_to_all | solution.py:287
  11.1 1.1 copy-start
  12.2 0.8 copy-start.4
  12.9 0.8 copy-start.8
  13.7 0.8 copy-start.11
  14.5 0.7 copy-start.14
  22.9 0.8 copy-start.5
  27.2 3.6 %collective-permute-start = (bf16[16,96,128]{2,1,0:T(8,128)(2,1)S(1)}, bf16[16,96,128]{2,1,0:T(8,128)(2,1)S(1)}, u32[]{:S(2)}, u32[]{:S(2)}) collective-permute-start(bf16[16,96,128]{2,1,0:T(8,128)(2,1)S(1)} %get-tuple-element.36), channel_id=1, source_target_pairs={{0,1},{1,0},{2,3},{3,2},{4,5},{5,4},{6,7},{7,6},{8,9},{9,8},{10,11... | collective-permute-start | bytes 1179656 | tf_op jit(solution)/shard_map/ppermute | solution.py:309
  31.6 37.4 %all-to-all-start.1 = ((bf16[16,96,128]{2,1,0:T(8,128)(2,1)}), bf16[16,96,128]{2,1,0:T(8,128)(2,1)S(1)}, u32[]{:S(2)}, u32[]{:S(2)}) async-start(bf16[16,96,128]{2,1,0:T(8,128)(2,1)} %add_convert_fusion), calls=%async_computation.1 | async-start | bytes 786432 | tf_op jit(solution)/shard_map/all_to_all | solution.py:311
  98.7 42.9 %copy-start.2 = (bf16[1,3072,384]{2,1,0:T(8,128)(2,1)S(1)}, bf16[1,3072,384]{2,1,0:T(8,128)(2,1)}, u32[]{:S(2)}) copy-start(bf16[1,3072,384]{2,1,0:T(8,128)(2,1)} %param.17) | copy-start | bytes 7077892
  98.7 42.9 %copy-start.3 = (bf16[1,384,3072]{2,1,0:T(8,128)(2,1)S(1)}, bf16[1,384,3072]{2,1,0:T(8,128)(2,1)}, u32[]{:S(2)}) copy-start(bf16[1,384,3072]{2,1,0:T(8,128)(2,1)} %param.18) | copy-start | bytes 7077892
  191.7 59.3 %copy-start.1 = (bf16[128,3072]{1,0:T(8,128)(2,1)S(1)}, bf16[128,3072]{1,0:T(8,128)(2,1)}, u32[]{:S(2)}) copy-start(bf16[128,3072]{1,0:T(8,128)(2,1)} %w_out.3) | copy-start | bytes 2359300
  191.7 59.3 %copy-start.6 = (bf16[128,128]{1,0:T(8,128)(2,1)S(1)}, bf16[128,128]{1,0:T(8,128)(2,1)}, u32[]{:S(2)}) copy-start(bf16[128,128]{1,0:T(8,128)(2,1)} %queries.7) | copy-start | bytes 98308
  192.4 65.1 %copy-start.9 = (bf16[128,128]{1,0:T(8,128)(2,1)S(1)}, bf16[128,128]{1,0:T(8,128)(2,1)}, u32[]{:S(2)}) copy-start(bf16[128,128]{1,0:T(8,128)(2,1)} %keys.7) | copy-start | bytes 98308
  192.4 65.1 %copy-start.12 = (bf16[128,128]{1,0:T(8,128)(2,1)S(1)}, bf16[128,128]{1,0:T(8,128)(2,1)}, u32[]{:S(2)}) copy-start(bf16[128,128]{1,0:T(8,128)(2,1)} %values.7) | copy-start | bytes 98308
  252.5 15.8 %all-to-all-start.6 = ((bf16[16,128,128]{2,1,0:T(8,128)(2,1)}), bf16[16,128,128]{2,1,0:T(8,128)(2,1)S(1)}, u32[]{:S(2)}, u32[]{:S(2)}) async-start(bf16[16,128,128]{2,1,0:T(8,128)(2,1)} %get-tuple-element.53), calls=%async_computation.6 | async-start | bytes 1048576 | tf_op jit(solution)/shard_map/all_to_all | solution.py:351

commit v3 on v2

v3 whole, which is shorter than its diff:
```python
import functools

import jax
import jax.numpy as jnp
from jax import lax
from jax.experimental import pallas as pl
from jax.experimental.pallas import tpu as pltpu
from jax.sharding import PartitionSpec as P

bf16 = jnp.bfloat16
f32 = jnp.float32
ROWS = 16


def mm(a, b, dims):
    return lax.dot_general(a, b, (dims, ((), ())), preferred_element_type=f32)


def mm_high(a, b, dims):
    return lax.dot_general(
        a, b, (dims, ((), ())), precision=lax.Precision.HIGHEST, preferred_element_type=f32
    )


def iota(shape, axis):
    return lax.broadcasted_iota(jnp.int32, shape, axis)


def turned(column):
    n = column.shape[0]
    return jnp.sum(jnp.where(iota((n, n), 0) == iota((n, n), 1), column, 0.0), axis=0, keepdims=True)


def run_kernel(body, outs, args, smem=0, raw=0, flops=10_000_000, moved=1_000_000, limit=24):
    vmem = pl.BlockSpec(memory_space=pltpu.VMEM)
    scalars = [pl.BlockSpec(memory_space=pltpu.SMEM)] * smem
    specs = scalars + [pl.BlockSpec()] * raw + [vmem] * (len(args) - smem - raw)
    return pl.pallas_call(
        body,
        out_shape=[jax.ShapeDtypeStruct(shape, dtype) for shape, dtype in outs],
        in_specs=specs,
        out_specs=[vmem] * len(outs),
        compiler_params=pltpu.CompilerParams(vmem_limit_bytes=limit << 20),
        cost_estimate=pl.CostEstimate(flops=flops, bytes_accessed=moved, transcendentals=0),
    )(*args)


def pack(left, right):
    both = jnp.concatenate([left, right], axis=2)
    lanes, half = 128, both.shape[1] // 2
    rest = both[:, :, lanes:]
    rest = jnp.concatenate([rest[:, :half], rest[:, half:]], axis=2)
    return jnp.concatenate([both[:, :, :lanes], rest], axis=1)


def unpack(rows, share):
    lanes, half = 128, rows.shape[1] // 3
    top, low = rows[:, : 2 * half], rows[:, 2 * half :]
    rest = lanes // 2
    low = jnp.concatenate([low[:, :, :rest], low[:, :, rest:]], axis=1)
    both = jnp.concatenate([top, low], axis=2)
    return both[:, :, :share], both[:, :, share:]


def running(decay_row):
    n = decay_row.shape[1]
    causal = iota((n, n), 0) >= iota((n, n), 1)
    return jnp.sum(jnp.where(causal, decay_row, 0.0), axis=1, keepdims=True)


def state_kernel(keys, values, log_decay, packed):
    cum = running(log_decay[...])
    n = cum.shape[0]
    last = cum[n - 1 :, :]
    kept = keys[...].astype(f32) * jnp.exp(last - cum)
    state = mm_high(kept, values[...].astype(f32), ((0,), (0,))).astype(bf16)
    dh = state.shape[1]
    high = last.astype(bf16).astype(f32)
    mid = (last - high).astype(bf16).astype(f32)
    low = last - high - mid
    row = iota((ROWS, dh), 0)
    tail = jnp.where(row == 0, high, jnp.where(row == 1, mid, jnp.where(row == 2, low, 0.0)))
    for block in range(packed.shape[0]):
        packed[block, :dh, :] = state
        packed[block, dh:, :] = tail.astype(bf16)


def inner_kernel(queries, keys, values, log_decay, w_out, scores, inner, decay, grow, keep, w_turned):
    cum = running(log_decay[...])
    n = cum.shape[0]
    causal = iota((n, n), 0) >= iota((n, n), 1)
    gaps = jnp.where(causal, cum - turned(cum), 0.0)
    fall = jnp.where(causal, jnp.exp(gaps), 0.0)
    pairs = mm_high(queries[...].astype(f32), keys[...].astype(f32), ((1,), (1,))) * fall
    scores[...] = pairs
    decay[...] = fall
    inner[...] = mm_high(pairs, values[...].astype(f32), ((1,), (0,)))
    grow[...] = jnp.broadcast_to(jnp.exp(cum), grow.shape)
    keep[...] = jnp.broadcast_to(jnp.exp(cum[n - 1 :, :] - cum), keep.shape)
    dh = w_out.shape[0]
    for start in range(0, w_out.shape[1], dh):
        w_turned[start : start + dh, :] = w_out[:, start : start + dh].astype(f32).T.astype(bf16)


def route_kernel(ids, weights, cotangent, picks, cot_parts, *, cap):
    _, tokens = ids.shape
    slots_all = picks.shape[0]
    experts = slots_all // cap
    chosen = [(ids[j : j + 1, :] == iota((experts, tokens), 0)).astype(f32) for j in range(2)]
    earlier = (iota((tokens, tokens), 0) < iota((tokens, tokens), 1)).astype(f32).astype(bf16)
    before = mm((chosen[0] + chosen[1]).astype(bf16), earlier, ((1,), (0,)))
    cot = cotangent[...].astype(f32)
    for j in range(2):
        slot = jnp.sum(before * chosen[j], axis=0, keepdims=True)
        position = ids[j : j + 1, :].astype(f32) * cap + slot
        down = iota((slots_all, tokens), 0).astype(f32)
        at = slice(j * tokens, (j + 1) * tokens)
        picks[:, at] = (position == down).astype(f32).astype(bf16)
        cot_parts[:, at] = (weights[j : j + 1, :] * cot).astype(bf16)


def heads_kernel(place, queries, arrived, inner, grow, w_turned, mine, other, incoming):
    me, core = place[0], lax.rem(place[1], 2)
    blocks = arrived.shape[0]
    dh = queries.shape[1]
    total = jnp.zeros((dh, dh), f32)
    gap = jnp.zeros((1, dh), f32)
    for block in reversed(range(blocks)):
        weight = jnp.where(block < me, jnp.exp(gap), 0.0)
        total = total + weight * arrived[block, :dh, :].astype(f32)
        last = jnp.sum(arrived[block, dh:, :].astype(f32), axis=0, keepdims=True)
        gap = gap + jnp.where(block < me, last, 0.0)
    incoming[...] = total
    outer = mm_high(queries[...].astype(f32), total, ((1,), (0,)))
    heads = (inner[...] + grow[...] * outer).astype(bf16)
    chips, share, _ = mine.shape
    partial = mm(w_turned[...], heads, ((1,), (1,))).astype(bf16)
    partial = partial.reshape(chips, 2, share, heads.shape[0])
    mine[...] = jnp.where(core == 0, partial[:, 0], partial[:, 1])
    other[...] = jnp.where(core == 0, partial[:, 1], partial[:, 0])


def send_kernel(resid, pieces, cot_parts, picks, residual, sent):
    attn = jnp.sum(pieces[...].astype(f32), axis=0).astype(bf16).astype(f32)
    total = (resid[...].astype(f32) + attn).astype(bf16)
    residual[...] = total
    tokens = total.shape[1]
    placed = picks[:, :tokens] + picks[:, tokens:]
    share = total.shape[0]
    experts, rows_each, _ = sent.shape
    cap = picks.shape[0] // experts
    rows = mm(placed, total, ((1,), (1,))).reshape(experts, cap, share)
    grads = mm(picks[...], cot_parts[...], ((1,), (1,))).reshape(experts, cap, share)
    sent[...] = pack(rows, grads).astype(bf16)


def norm_kernel(rows, packed, own, rstd_out):
    experts = rows.shape[0]
    blocks, both, width = packed.shape
    cap, share = both // 2, width // experts
    left, right = unpack(rows[...].astype(f32), share)
    whole = jnp.concatenate([left[e] for e in range(experts)], axis=1)
    grads = jnp.concatenate([right[e] for e in range(experts)], axis=1).astype(bf16)
    rstd = lax.rsqrt(jnp.sum(whole * whole, axis=1, keepdims=True) / width + 1e-6)
    own[...] = whole.astype(bf16)
    rstd_out[...] = jnp.broadcast_to(rstd, rstd_out.shape)
    normed = (whole * rstd).astype(bf16)
    for block in range(blocks):
        packed[block, :cap, :] = normed
        packed[block, cap:, :] = grads


def expert_kernel(w_up, w_down, everyone, sums, *, step):
    blocks, both, width = everyone.shape
    cap = both // 2
    rows = blocks * cap
    hidden = w_up.shape[1]
    upper = jnp.zeros((rows, hidden), f32)
    grad_act = jnp.zeros((rows, hidden), f32)
    for start in range(0, width, step):
        at = slice(start, start + step)
        x = everyone[:, :cap, at].reshape(rows, step)
        g = everyone[:, cap:, at].reshape(rows, step)
        upper = upper + mm(x, w_up[at, :], ((1,), (0,)))
        grad_act = grad_act + mm(g, w_down[:, at], ((1,), (1,)))
    sigma = 1.0 / (1.0 + jnp.exp(-upper))
    act = (upper * sigma).astype(bf16)
    grad_up = (grad_act * (sigma * (1.0 + upper * (1.0 - sigma)))).astype(bf16)
    for start in range(0, width, step):
        at = slice(start, start + step)
        out = mm(act, w_down[:, at], ((1,), (0,))).astype(bf16)
        back = mm(grad_up, w_up[at, :], ((1,), (1,))).astype(bf16)
        sums[:, :cap, at] = out.reshape(blocks, cap, step)
        sums[:, cap:, at] = back.reshape(blocks, cap, step)


def back_kernel(sums, own, rstd_in, returned):
    experts = returned.shape[0]
    total = jnp.sum(sums[...].astype(f32), axis=0)
    cap, width = own.shape
    share = width // experts
    out, grads = total[:cap], total[cap:].astype(bf16).astype(f32)
    rows = own[...].astype(f32)
    rstd = rstd_in[:, :1]
    inner = jnp.sum(grads * rows, axis=1, keepdims=True)
    grads = rstd * grads - rows * (rstd * rstd * rstd * inner / width)
    left = jnp.stack([out[:, e * share : (e + 1) * share] for e in range(experts)])
    right = jnp.stack([grads[:, e * share : (e + 1) * share] for e in range(experts)])
    returned[...] = pack(left, right).astype(bf16)


def join_kernel(returned, picks, weights, residual, cotangent, layer_out, resid_grad):
    share, tokens = residual.shape
    slots_all = picks.shape[0]
    left, right = unpack(returned[...].astype(f32), share)
    left = left.reshape(slots_all, share).astype(bf16)
    right = right.reshape(slots_all, share).astype(bf16)
    both = mm(left, picks[...], ((0,), (0,)))
    routed = weights[0:1, :] * both[:, :tokens] + weights[1:2, :] * both[:, tokens:]
    layer_out[...] = (residual[...].astype(f32) + routed).astype(bf16)
    placed = picks[:, :tokens] + picks[:, tokens:]
    summed = mm(right, placed, ((0,), (0,)))
    resid_grad[...] = (cotangent[...].astype(f32) + summed).astype(bf16)


def state_grad_kernel(w_out, queries, turned_grads, grow, grad_heads, packed):
    flipped = mm(w_out[...], turned_grads[...], ((1,), (0,)))
    grads = flipped.T
    grad_heads[...] = grads
    state = mm_high(queries[...].astype(f32) * grow[...], grads, ((0,), (0,))).astype(bf16)
    for block in range(packed.shape[0]):
        packed[block] = state


def grads_kernel(
    queries, keys, values, grad_heads, scores, decay, grow, incoming, q_grad, k_part, v_part
):
    grads = grad_heads[...]
    score_grad = mm_high(grads, values[...].astype(f32), ((1,), (1,))) * decay[...]
    direct = mm_high(score_grad, keys[...].astype(f32), ((1,), (0,)))
    carried = mm_high(grads, incoming[...], ((1,), (1,)))
    q_grad[...] = (direct + grow[...] * carried).astype(bf16)
    k_part[...] = mm_high(score_grad, queries[...].astype(f32), ((0,), (0,)))
    v_part[...] = mm_high(scores[...], grads, ((0,), (0,)))


def last_kernel(place, keys, values, arrived, tails, keep, k_part, v_part, k_grad, v_grad):
    me = place[0]
    blocks, dh, _ = arrived.shape
    total = jnp.zeros((dh, dh), f32)
    gap = jnp.zeros((1, dh), f32)
    for block in range(blocks):
        weight = jnp.where(block > me, jnp.exp(gap), 0.0)
        total = total + weight * arrived[block].astype(f32)
        last = jnp.sum(tails[block, dh:, :].astype(f32), axis=0, keepdims=True)
        gap = gap + jnp.where(block > me, last, 0.0)
    from_values = mm_high(values[...].astype(f32), total, ((1,), (1,)))
    from_keys = mm_high(keys[...].astype(f32), total, ((1,), (0,)))
    k_grad[...] = (k_part[...] + keep[...] * from_values).astype(bf16)
    v_grad[...] = (v_part[...] + keep[...] * from_keys).astype(bf16)


def local(
    resid, queries, keys, values, log_decay, w_out, w_up, w_down, expert_ids, route_weights, cotangent
):
    n_ctx, n_exp = lax.axis_size("ctx"), lax.axis_size("exp")
    chips = n_exp // 2
    place = jnp.stack([lax.axis_index("ctx"), lax.axis_index("exp")]).astype(jnp.int32)
    tokens, dh = queries.shape
    width = w_out.shape[1]
    share = width // n_exp
    cap = 4 * tokens // n_exp
    partner = [(i, i ^ 1) for i in range(n_exp)]
    same_core = [[2 * z + c for z in range(chips)] for c in range(2)]
    square = (tokens, dh)
    flat = (share, tokens)
    weights, cot = route_weights.T, cotangent.T
    packed_rows = (n_exp, cap * 2 * share // 128, 128)

    [packed] = run_kernel(
        state_kernel, [((n_ctx, dh + ROWS, dh), bf16)], (keys, values, log_decay), raw=3
    )
    arrived = lax.all_to_all(packed, "ctx", 0, 0)
    scores, inner, decay, grow, keep, w_turned = run_kernel(
        inner_kernel,
        [((tokens, tokens), f32), (square, f32), ((tokens, tokens), f32), (square, f32), (square, f32)]
        + [((width, dh), bf16)],
        (queries, keys, values, log_decay, w_out),
        raw=5,
    )
    picks, cot_parts = run_kernel(
        functools.partial(route_kernel, cap=cap),
        [((n_exp * cap, 2 * tokens), bf16), ((share, 2 * tokens), bf16)],
        (expert_ids.T, weights, cot),
        raw=3,
    )
    mine, other, incoming = run_kernel(
        heads_kernel,
        [((chips, share, tokens), bf16)] * 2 + [((dh, dh), f32)],
        (place, queries, arrived, inner, grow, w_turned),
        smem=1,
        raw=1,
    )
    other = lax.ppermute(other, "exp", partner)
    pair = (mine.astype(f32) + other.astype(f32)).astype(bf16)
    pieces = lax.all_to_all(pair, "exp", 0, 0, axis_index_groups=same_core)
    residual, sent = run_kernel(
        send_kernel,
        [(flat, bf16), (packed_rows, bf16)],
        (resid.T, pieces, cot_parts, picks),
        raw=1,
    )
    rows = lax.all_to_all(sent, "exp", 0, 0)
    packed, own, rstd = run_kernel(
        norm_kernel,
        [((n_ctx, 2 * cap, width), bf16), ((cap, width), bf16), ((cap, 128), f32)],
        (rows,),
    )
    everyone = lax.all_to_all(packed, "ctx", 0, 0)
    [sums] = run_kernel(
        functools.partial(expert_kernel, step=512 if width % 512 == 0 else 384),
        [((n_ctx, 2 * cap, width), bf16)],
        (w_up[0], w_down[0], everyone),
        flops=2_400_000_000,
        moved=11_000_000,
    )
    sums = lax.all_to_all(sums, "ctx", 0, 0)
    [returned] = run_kernel(back_kernel, [(packed_rows, bf16)], (sums, own, rstd))
    returned = lax.all_to_all(returned, "exp", 0, 0)
    layer_out, resid_grad = run_kernel(
        join_kernel,
        [(flat, bf16), (flat, bf16)],
        (returned, picks, weights, residual, cot),
    )
    turned_grads = lax.all_gather(resid_grad, "exp", tiled=True)
    grad_heads, packed = run_kernel(
        state_grad_kernel,
        [(square, f32), ((n_ctx, dh, dh), bf16)],
        (w_out, queries, turned_grads, grow),
    )
    states = lax.all_to_all(packed, "ctx", 0, 0)
    q_grad, k_part, v_part = run_kernel(
        grads_kernel,
        [(square, bf16), (square, f32), (square, f32)],
        (queries, keys, values, grad_heads, scores, decay, grow, incoming),
    )
    k_grad, v_grad = run_kernel(
        last_kernel,
        [(square, bf16), (square, bf16)],
        (place, keys, values, states, arrived, keep, k_part, v_part),
        smem=1,
    )
    return layer_out.T, resid_grad.T, q_grad, k_grad, v_grad


def solution(mesh):
    both = P("ctx", "exp")
    rows = P("ctx", None)
    return jax.shard_map(
        local,
        mesh=mesh,
        in_specs=(
            both, both, both, both, P("exp", "ctx"), P("exp", None),
            P("exp", None, "ctx"), P("exp", "ctx", None), rows, rows, both,
        ),
        out_specs=(both,) * 5,
        check_vma=False,
    )
```

time: 271 us -> 259 us (0.956)
  Pallas kernels: 20.3 us -> 13.7 us
  blocking collectives: 172 us -> 166 us
    pallas_call x12, Pallas kernels: 20.3 us -> 13.7 us  [run_kernel(): pl.pallas_call(body, out_shape=[jax.ShapeDtypeStruct(shape, dtype) for sh...]
    all_to_all x1, blocking collectives: 27.2 us -> 24.2 us  [local(): returned = lax.all_to_all(returned, 'exp', 0, 0)]
    unnamed x44 -> x38, local copies, waits for them, and re-layouts: 8.89 us -> 7.02 us
  transfers between devices with their start and end apart: 4 -> 4, of which waited for: 4 -> 4; matrix products, arithmetic and copies ran while one was open for 1% -> 0% of each run, Pallas kernels for 1% -> 1%
where the time goes in v3:
time: 259 us; the launch traced here: 258 us
  blocking collectives  166 us (64%)
  waiting for transfers between devices  41.7 us (16%)
  starting transfers between devices  28.2 us (11%)
  Pallas kernels  13.7 us (5%)
  local copies, waits for them, and re-layouts  7.02 us (3%)
    all_to_all x1, blocking collectives, local(): everyone = lax.all_to_all(packed, 'ctx', 0, 0)  42.9 us
    all_to_all x1, blocking collectives, local(): sums = lax.all_to_all(sums, 'ctx', 0, 0)  41.5 us
    all_gather x1, blocking collectives, local(): turned_grads = lax.all_gather(resid_grad, 'exp', tiled=True)  31 us
    all_to_all x1, blocking collectives, local(): rows = lax.all_to_all(sent, 'exp', 0, 0)  26.2 us
    all_to_all x1, blocking collectives, local(): returned = lax.all_to_all(returned, 'exp', 0, 0)  24.2 us
    all_to_all x1, waiting for transfers between devices, local(): pieces = lax.all_to_all(pair, 'exp', 0, 0, axis_index_groups=same_core)  21.9 us
    all_to_all x1, starting transfers between devices, local(): pieces = lax.all_to_all(pair, 'exp', 0, 0, axis_index_groups=same_core)  15.2 us
    pallas_call x12, Pallas kernels, run_kernel(): pl.pallas_call(body, out_shape=[jax.ShapeDtypeStruct(shape, dtype) for sh...  13.7 us
  transfers between devices with their start and end apart: 4, of which 4 were waited for; matrix products, arithmetic and copies ran while one was open for 0% of the time, Pallas kernels for 1%

profile of v3, /device:TPU:32, one launch (start us, length us, event | category | flops | bytes accessed | tf_op | source)
XLA Modules:
  0.0 258.1 jit_solution(5548906738224926610)
XLA Ops:
  2.8 1.2 shard_map.146
  4.0 7.0 %all-to-all-start = ((bf16[16,144,128]{2,1,0:T(8,128)(2,1)}), bf16[16,144,128]{2,1,0:T(8,128)(2,1)S(1)}, u32[]{:S(2)}, u32[]{:S(2)}) async-start(bf16[16,144,128]{2,1,0:T(8,128)(2,1)} %shard_map.146), calls=%async_computation | async-start | bytes 1179648 | tf_op jit(solution)/shard_map/all_to_all | solution.py:283
  11.1 1.1 copy-done
  15.7 7.2 %all-to-all-done.arrived.tails = bf16[16,144,128]{2,1,0:T(8,128)(2,1)S(1)} async-done(((bf16[16,144,128]{2,1,0:T(8,128)(2,1)}), bf16[16,144,128]{2,1,0:T(8,128)(2,1)S(1)}, u32[]{:S(2)}, u32[]{:S(2)}) %all-to-all-start) | async-done | bytes 589856 | tf_op jit(solution)/shard_map/all_to_all | solution.py:283
  22.9 0.8 copy-done.5
  23.7 1.3 shard_map.148
  25.0 1.9 collective-permute-start
  26.9 1.7 collective-permute-done
  28.6 0.8 add_convert_fusion
  29.5 15.2 %all-to-all-start.1 = ((bf16[16,96,128]{2,1,0:T(8,128)(2,1)}), bf16[16,96,128]{2,1,0:T(8,128)(2,1)S(1)}, u32[]{:S(2)}, u32[]{:S(2)}) async-start(bf16[16,96,128]{2,1,0:T(8,128)(2,1)} %add_convert_fusion), calls=%async_computation.1 | async-start | bytes 786432 | tf_op jit(solution)/shard_map/all_to_all | solution.py:306
  44.9 21.9 %all-to-all-done.1.pieces = bf16[16,96,128]{2,1,0:T(8,128)(2,1)S(1)} async-done(((bf16[16,96,128]{2,1,0:T(8,128)(2,1)}), bf16[16,96,128]{2,1,0:T(8,128)(2,1)S(1)}, u32[]{:S(2)}, u32[]{:S(2)}) %all-to-all-start.1) | async-done | bytes 393248 | tf_op jit(solution)/shard_map/all_to_all | solution.py:306
  67.3 26.2 %all_to_all.35.rows = bf16[32,24,128]{2,1,0:T(8,128)(2,1)S(1)} all-to-all(bf16[32,24,128]{2,1,0:T(8,128)(2,1)S(1)} %get-tuple-element.37), channel_id=1, replica_groups=mesh['ctx'=16,'exp'=32] {'exp'}, dimensions={0} | all-to-all | bytes 393216 | tf_op jit(solution)/shard_map/all_to_all | solution.py:313
  93.9 42.9 %all_to_all.36.everyone = bf16[16,32,3072]{2,1,0:T(8,128)(2,1)S(1)} all-to-all(bf16[16,32,3072]{2,1,0:T(8,128)(2,1)S(1)} %get-tuple-element.38), channel_id=1, replica_groups=mesh['ctx'=16,'exp'=32] {'ctx'}, dimensions={0} | all-to-all | bytes 6291456 | tf_op jit(solution)/shard_map/all_to_all | solution.py:319
  136.8 3.4 %shard_map.152 = bf16[16,32,3072]{2,1,0:T(8,128)(2,1)S(1)} custom-call(bf16[3072,384]{1,0:T(8,128)(2,1)S(1)} %bitcast.10, bf16[384,3072]{1,0:T(8,128)(2,1)S(1)} %bitcast.11, bf16[16,32,3072]{2,1,0:T(8,128)(2,1)S(1)} %all_to_all.36.everyone), custom_call_target="tpu_custom_call" | custom-call | flops 2400000000 | bytes 11000000 | tf_op jit(solution)/shard_map/pallas_call | solution.py:38
  140.3 41.5 %all_to_all.37.sums = bf16[16,32,3072]{2,1,0:T(8,128)(2,1)S(1)} all-to-all(bf16[16,32,3072]{2,1,0:T(8,128)(2,1)S(1)} %shard_map.152), channel_id=1, replica_groups=mesh['ctx'=16,'exp'=32] {'ctx'}, dimensions={0} | all-to-all | bytes 6291456 | tf_op jit(solution)/shard_map/all_to_all | solution.py:327
  181.8 0.8 shard_map.153
  182.7 24.2 %all_to_all.38.returned = bf16[32,24,128]{2,1,0:T(8,128)(2,1)S(1)} all-to-all(bf16[32,24,128]{2,1,0:T(8,128)(2,1)S(1)} %shard_map.153), channel_id=1, replica_groups=mesh['ctx'=16,'exp'=32] {'exp'}, dimensions={0} | all-to-all | bytes 393216 | tf_op jit(solution)/shard_map/all_to_all | solution.py:329
  206.9 1.0 shard_map.154
  207.9 31.0 %all_gather.3.turned_grads = bf16[3072,128]{1,0:T(8,128)(2,1)S(1)} all-gather(bf16[96,128]{1,0:T(8,128)(2,1)} %get-tuple-element.43), channel_id=1, replica_groups=mesh['ctx'=16,'exp'=32] {'exp'}, dimensions={0}, use_global_device_ids=true | all-gather | bytes 811008 | tf_op jit(solution)/shard_map/all_gather | solution.py:335
  238.9 1.5 shard_map.155
  240.5 4.0 %all-to-all-start.6 = ((bf16[16,128,128]{2,1,0:T(8,128)(2,1)}), bf16[16,128,128]{2,1,0:T(8,128)(2,1)S(1)}, u32[]{:S(2)}, u32[]{:S(2)}) async-start(bf16[16,128,128]{2,1,0:T(8,128)(2,1)} %get-tuple-element.49), calls=%async_computation.6 | async-start | bytes 1048576 | tf_op jit(solution)/shard_map/all_to_all | solution.py:341
  244.5 1.2 shard_map.156
  245.7 10.8 %all-to-all-done.6.arrived = bf16[16,128,128]{2,1,0:T(8,128)(2,1)S(1)} async-done(((bf16[16,128,128]{2,1,0:T(8,128)(2,1)}), bf16[16,128,128]{2,1,0:T(8,128)(2,1)S(1)}, u32[]{:S(2)}, u32[]{:S(2)}) %all-to-all-start.6) | async-done | bytes 524320 | tf_op jit(solution)/shard_map/all_to_all | solution.py:341
  256.5 1.6 shard_map.157
  (41 shorter events, 6.8 us)
Async XLA Ops:
  0.6 0.8 copy-start.7
  1.4 0.8 copy-start.10
  2.2 0.7 copy-start.15
  2.8 41.9 %copy-start.14 = (bf16[128,96]{0,1:T(8,128)(2,1)S(1)}, bf16[128,96]{0,1:T(8,128)(2,1)}, u32[]{:S(2)}) copy-start(bf16[128,96]{0,1:T(8,128)(2,1)} %param.21) | copy-start | bytes 73732
  2.8 41.9 %copy-start.17 = (f32[128,2]{0,1:T(2,128)S(1)}, f32[128,2]{0,1:T(2,128)}, u32[]{:S(2)}) copy-start(f32[128,2]{0,1:T(2,128)} %param.20) | copy-start | bytes 3076
  2.8 41.9 %copy-start.18 = (s32[128,2]{0,1:T(2,128)S(1)}, s32[128,2]{0,1:T(2,128)}, u32[]{:S(2)}) copy-start(s32[128,2]{0,1:T(2,128)} %param.19) | copy-start | bytes 3076
  2.8 64.1 %copy-start.13 = (bf16[128,96]{0,1:T(8,128)(2,1)S(1)}, bf16[128,96]{0,1:T(8,128)(2,1)}, u32[]{:S(2)}) copy-start(bf16[128,96]{0,1:T(8,128)(2,1)} %param.11) | copy-start | bytes 73732
  4.0 18.9 %all-to-all-start = ((bf16[16,144,128]{2,1,0:T(8,128)(2,1)}), bf16[16,144,128]{2,1,0:T(8,128)(2,1)S(1)}, u32[]{:S(2)}, u32[]{:S(2)}) async-start(bf16[16,144,128]{2,1,0:T(8,128)(2,1)} %shard_map.146), calls=%async_computation | async-start | bytes 1179648 | tf_op jit(solution)/shard_map/all_to_all | solution.py:283
  11.1 1.1 copy-start
  12.2 0.8 copy-start.4
  12.9 0.8 copy-start.8
  13.7 0.8 copy-start.11
  14.5 0.7 copy-start.16
  22.9 0.8 copy-start.5
  25.0 3.6 %collective-permute-start = (bf16[16,96,128]{2,1,0:T(8,128)(2,1)S(1)}, bf16[16,96,128]{2,1,0:T(8,128)(2,1)S(1)}, u32[]{:S(2)}, u32[]{:S(2)}) collective-permute-start(bf16[16,96,128]{2,1,0:T(8,128)(2,1)S(1)} %get-tuple-element.34), channel_id=1, source_target_pairs={{0,1},{1,0},{2,3},{3,2},{4,5},{5,4},{6,7},{7,6},{8,9},{9,8},{10,11... | collective-permute-start | bytes 1179656 | tf_op jit(solution)/shard_map/ppermute | solution.py:304
  29.5 37.4 %all-to-all-start.1 = ((bf16[16,96,128]{2,1,0:T(8,128)(2,1)}), bf16[16,96,128]{2,1,0:T(8,128)(2,1)S(1)}, u32[]{:S(2)}, u32[]{:S(2)}) async-start(bf16[16,96,128]{2,1,0:T(8,128)(2,1)} %add_convert_fusion), calls=%async_computation.1 | async-start | bytes 786432 | tf_op jit(solution)/shard_map/all_to_all | solution.py:306
  93.9 43.0 %copy-start.2 = (bf16[1,3072,384]{2,1,0:T(8,128)(2,1)S(1)}, bf16[1,3072,384]{2,1,0:T(8,128)(2,1)}, u32[]{:S(2)}) copy-start(bf16[1,3072,384]{2,1,0:T(8,128)(2,1)} %param.17) | copy-start | bytes 7077892
  93.9 43.0 %copy-start.3 = (bf16[1,384,3072]{2,1,0:T(8,128)(2,1)S(1)}, bf16[1,384,3072]{2,1,0:T(8,128)(2,1)}, u32[]{:S(2)}) copy-start(bf16[1,384,3072]{2,1,0:T(8,128)(2,1)} %param.18) | copy-start | bytes 7077892
  181.8 57.1 %copy-start.1 = (bf16[128,3072]{1,0:T(8,128)(2,1)S(1)}, bf16[128,3072]{1,0:T(8,128)(2,1)}, u32[]{:S(2)}) copy-start(bf16[128,3072]{1,0:T(8,128)(2,1)} %w_out.3) | copy-start | bytes 2359300
  181.8 57.1 %copy-start.6 = (bf16[128,128]{1,0:T(8,128)(2,1)S(1)}, bf16[128,128]{1,0:T(8,128)(2,1)}, u32[]{:S(2)}) copy-start(bf16[128,128]{1,0:T(8,128)(2,1)} %queries.7) | copy-start | bytes 98308
  181.8 62.7 %copy-start.9 = (bf16[128,128]{1,0:T(8,128)(2,1)S(1)}, bf16[128,128]{1,0:T(8,128)(2,1)}, u32[]{:S(2)}) copy-start(bf16[128,128]{1,0:T(8,128)(2,1)} %keys.7) | copy-start | bytes 98308
  181.8 62.7 %copy-start.12 = (bf16[128,128]{1,0:T(8,128)(2,1)S(1)}, bf16[128,128]{1,0:T(8,128)(2,1)}, u32[]{:S(2)}) copy-start(bf16[128,128]{1,0:T(8,128)(2,1)} %values.7) | copy-start | bytes 98308
  240.5 16.0 %all-to-all-start.6 = ((bf16[16,128,128]{2,1,0:T(8,128)(2,1)}), bf16[16,128,128]{2,1,0:T(8,128)(2,1)S(1)}, u32[]{:S(2)}, u32[]{:S(2)}) async-start(bf16[16,128,128]{2,1,0:T(8,128)(2,1)} %get-tuple-element.49), calls=%async_computation.6 | async-start | bytes 1048576 | tf_op jit(solution)/shard_map/all_to_all | solution.py:341

commit v4 on v3

--- a/solution.py
+++ b/solution.py
@@ -1,4 +1,5 @@
 import functools
+import math
 
 import jax
 import jax.numpy as jnp
@@ -31,15 +32,20 @@
     return jnp.sum(jnp.where(iota((n, n), 0) == iota((n, n), 1), column, 0.0), axis=0, keepdims=True)
 
 
-def run_kernel(body, outs, args, smem=0, raw=0, flops=10_000_000, moved=1_000_000, limit=24):
+def run_kernel(
+    body, outs, args, smem=0, raw=0, far=0, scratch=(), flops=10_000_000, moved=1_000_000, limit=24
+):
     vmem = pl.BlockSpec(memory_space=pltpu.VMEM)
     scalars = [pl.BlockSpec(memory_space=pltpu.SMEM)] * smem
-    specs = scalars + [pl.BlockSpec()] * raw + [vmem] * (len(args) - smem - raw)
+    hbm = pl.BlockSpec(memory_space=pltpu.HBM)
+    near = len(args) - smem - far - raw
+    specs = scalars + [hbm] * far + [pl.BlockSpec()] * raw + [vmem] * near
     return pl.pallas_call(
         body,
         out_shape=[jax.ShapeDtypeStruct(shape, dtype) for shape, dtype in outs],
         in_specs=specs,
         out_specs=[vmem] * len(outs),
+        scratch_shapes=scratch,
         compiler_params=pltpu.CompilerParams(vmem_limit_bytes=limit << 20),
         cost_estimate=pl.CostEstimate(flops=flops, bytes_accessed=moved, transcendentals=0),
     )(*args)
@@ -68,7 +74,13 @@
     return jnp.sum(jnp.where(causal, decay_row, 0.0), axis=1, keepdims=True)
 
 
-def state_kernel(keys, values, log_decay, packed):
+def state_kernel(keys_far, values_far, decay_far, packed, keys, values, log_decay, arrivals):
+    pairs = ((keys_far, keys), (values_far, values), (decay_far, log_decay))
+    copies = [pltpu.make_async_copy(a, b, arrivals.at[i]) for i, (a, b) in enumerate(pairs)]
+    for copy in copies:
+        copy.start()
+    for copy in copies:
+        copy.wait()
     cum = running(log_decay[...])
     n = cum.shape[0]
     last = cum[n - 1 :, :]
@@ -85,7 +97,7 @@
         packed[block, dh:, :] = tail.astype(bf16)
 
 
-def inner_kernel(queries, keys, values, log_decay, w_out, scores, inner, decay, grow, keep, w_turned):
+def inner_kernel(queries, keys, values, log_decay, w_out, scores, inner, decay, grow, keep, grown, w_turned):
     cum = running(log_decay[...])
     n = cum.shape[0]
     causal = iota((n, n), 0) >= iota((n, n), 1)
@@ -96,6 +108,7 @@
     decay[...] = fall
     inner[...] = mm_high(pairs, values[...].astype(f32), ((1,), (0,)))
     grow[...] = jnp.broadcast_to(jnp.exp(cum), grow.shape)
+    grown[...] = queries[...].astype(f32) * jnp.exp(cum)
     keep[...] = jnp.broadcast_to(jnp.exp(cum[n - 1 :, :] - cum), keep.shape)
     dh = w_out.shape[0]
     for start in range(0, w_out.shape[1], dh):
@@ -119,10 +132,10 @@
         cot_parts[:, at] = (weights[j : j + 1, :] * cot).astype(bf16)
 
 
-def heads_kernel(place, queries, arrived, inner, grow, w_turned, mine, other, incoming):
+def heads_kernel(place, arrived, inner, grown, w_turned, mine, other, incoming):
     me, core = place[0], lax.rem(place[1], 2)
     blocks = arrived.shape[0]
-    dh = queries.shape[1]
+    dh = grown.shape[1]
     total = jnp.zeros((dh, dh), f32)
     gap = jnp.zeros((1, dh), f32)
     for block in reversed(range(blocks)):
@@ -131,8 +144,7 @@
         last = jnp.sum(arrived[block, dh:, :].astype(f32), axis=0, keepdims=True)
         gap = gap + jnp.where(block < me, last, 0.0)
     incoming[...] = total
-    outer = mm_high(queries[...].astype(f32), total, ((1,), (0,)))
-    heads = (inner[...] + grow[...] * outer).astype(bf16)
+    heads = (inner[...] + mm_high(grown[...], total, ((1,), (0,)))).astype(bf16)
     chips, share, _ = mine.shape
     partial = mm(w_turned[...], heads, ((1,), (1,))).astype(bf16)
     partial = partial.reshape(chips, 2, share, heads.shape[0])
@@ -194,6 +206,13 @@
         sums[:, cap:, at] = back.reshape(blocks, cap, step)
 
 
+def half_kernel(sums, out, *, step):
+    for start in range(0, out.shape[2], step):
+        at = slice(start, start + step)
+        total = jnp.sum(sums[:, :, at].astype(f32), axis=0).astype(bf16)
+        out[:, :, at] = total.reshape(out.shape[0], out.shape[1], step)
+
+
 def back_kernel(sums, own, rstd_in, returned):
     experts = returned.shape[0]
     total = jnp.sum(sums[...].astype(f32), axis=0)
@@ -223,11 +242,11 @@
     resid_grad[...] = (cotangent[...].astype(f32) + summed).astype(bf16)
 
 
-def state_grad_kernel(w_out, queries, turned_grads, grow, grad_heads, packed):
+def state_grad_kernel(w_out, turned_grads, grown, grad_heads, packed):
     flipped = mm(w_out[...], turned_grads[...], ((1,), (0,)))
     grads = flipped.T
     grad_heads[...] = grads
-    state = mm_high(queries[...].astype(f32) * grow[...], grads, ((0,), (0,))).astype(bf16)
+    state = mm_high(grown[...], grads, ((0,), (0,))).astype(bf16)
     for block in range(packed.shape[0]):
         packed[block] = state
 
@@ -272,19 +291,32 @@
     cap = 4 * tokens // n_exp
     partner = [(i, i ^ 1) for i in range(n_exp)]
     same_core = [[2 * z + c for z in range(chips)] for c in range(2)]
+    side = math.isqrt(n_ctx)
+    axes = ("ctx", "exp")
+    first, second = [], []
+    for e in range(n_exp):
+        along_y = [[(x * side + y) * n_exp + e for y in range(side)] for x in range(side)]
+        along_x = [[(x * side + y) * n_exp + e for x in range(side)] for y in range(side)]
+        first += along_x if e % 2 else along_y
+        second += along_y if e % 2 else along_x
     square = (tokens, dh)
     flat = (share, tokens)
     weights, cot = route_weights.T, cotangent.T
     packed_rows = (n_exp, cap * 2 * share // 128, 128)
 
     [packed] = run_kernel(
-        state_kernel, [((n_ctx, dh + ROWS, dh), bf16)], (keys, values, log_decay), raw=3
+        state_kernel,
+        [((n_ctx, dh + ROWS, dh), bf16)],
+        (keys, values, log_decay),
+        far=3,
+        scratch=[pltpu.VMEM(square, bf16)] * 2
+        + [pltpu.VMEM(log_decay.shape, f32), pltpu.SemaphoreType.DMA((3,))],
     )
     arrived = lax.all_to_all(packed, "ctx", 0, 0)
-    scores, inner, decay, grow, keep, w_turned = run_kernel(
+    scores, inner, decay, grow, keep, grown, w_turned = run_kernel(
         inner_kernel,
         [((tokens, tokens), f32), (square, f32), ((tokens, tokens), f32), (square, f32), (square, f32)]
-        + [((width, dh), bf16)],
+        + [(square, f32), ((width, dh), bf16)],
         (queries, keys, values, log_decay, w_out),
         raw=5,
     )
@@ -297,9 +329,8 @@
     mine, other, incoming = run_kernel(
         heads_kernel,
         [((chips, share, tokens), bf16)] * 2 + [((dh, dh), f32)],
-        (place, queries, arrived, inner, grow, w_turned),
+        (place, arrived, inner, grown, w_turned),
         smem=1,
-        raw=1,
     )
     other = lax.ppermute(other, "exp", partner)
     pair = (mine.astype(f32) + other.astype(f32)).astype(bf16)
@@ -313,10 +344,13 @@
     rows = lax.all_to_all(sent, "exp", 0, 0)
     packed, own, rstd = run_kernel(
         norm_kernel,
-        [((n_ctx, 2 * cap, width), bf16), ((cap, width), bf16), ((cap, 128), f32)],
+        [((side, 2 * cap, width), bf16), ((cap, width), bf16), ((cap, 128), f32)],
         (rows,),
     )
-    everyone = lax.all_to_all(packed, "ctx", 0, 0)
+    line = lax.all_to_all(packed, axes, 0, 0, axis_index_groups=first)
+    line = jnp.broadcast_to(line.reshape(1, side * 2 * cap, width), (side, side * 2 * cap, width))
+    everyone = lax.all_to_all(line, axes, 0, 0, axis_index_groups=second)
+    everyone = everyone.reshape(n_ctx, 2 * cap, width)
     [sums] = run_kernel(
         functools.partial(expert_kernel, step=512 if width % 512 == 0 else 384),
         [((n_ctx, 2 * cap, width), bf16)],
@@ -324,7 +358,12 @@
         flops=2_400_000_000,
         moved=11_000_000,
     )
-    sums = lax.all_to_all(sums, "ctx", 0, 0)
+    sums = sums.reshape(side, side * 2 * cap, width)
+    sums = lax.all_to_all(sums, axes, 0, 0, axis_index_groups=second)
+    [sums] = run_kernel(
+        functools.partial(half_kernel, step=128), [((side, 2 * cap, width), bf16)], (sums,)
+    )
+    sums = lax.all_to_all(sums, axes, 0, 0, axis_index_groups=first)
     [returned] = run_kernel(back_kernel, [(packed_rows, bf16)], (sums, own, rstd))
     returned = lax.all_to_all(returned, "exp", 0, 0)
     layer_out, resid_grad = run_kernel(
@@ -336,7 +375,7 @@
     grad_heads, packed = run_kernel(
         state_grad_kernel,
         [(square, f32), ((n_ctx, dh, dh), bf16)],
-        (w_out, queries, turned_grads, grow),
+        (w_out, turned_grads, grown),
     )
     states = lax.all_to_all(packed, "ctx", 0, 0)
     q_grad, k_part, v_part = run_kernel(

time: 259 us -> 247 us (0.954)
  blocking collectives: 166 us -> 154 us
    all_to_all x2 -> x4, blocking collectives: 84.4 us -> 73.7 us  [the longest x1 25 us: local(): everyone = lax.all_to_all(line, axes, 0, 0, axis_index_groups=second)]
    unnamed x38 -> x36, local copies, waits for them, and re-layouts: 7.02 us -> 6.27 us
    pallas_call x12 -> x13, Pallas kernels: 13.7 us -> 13.8 us  [run_kernel(): pl.pallas_call(body, out_shape=[jax.ShapeDtypeStruct(shape, dtype) for sh...]
where the time goes in v4:
time: 247 us; the launch traced here: 246 us
  blocking collectives  154 us (62%)
  waiting for transfers between devices  41.9 us (17%)
  starting transfers between devices  27.7 us (11%)
  Pallas kernels  13.8 us (6%)
  local copies, waits for them, and re-layouts  6.63 us (3%)
    all_gather x1, blocking collectives, local(): turned_grads = lax.all_gather(resid_grad, 'exp', tiled=True)  30.9 us
    all_to_all x1, blocking collectives, local(): rows = lax.all_to_all(sent, 'exp', 0, 0)  26.2 us
    all_to_all x1, blocking collectives, local(): everyone = lax.all_to_all(line, axes, 0, 0, axis_index_groups=second)  25 us
    all_to_all x1, blocking collectives, local(): sums = lax.all_to_all(sums, axes, 0, 0, axis_index_groups=second)  24.6 us
    all_to_all x1, blocking collectives, local(): returned = lax.all_to_all(returned, 'exp', 0, 0)  23.1 us
    all_to_all x1, waiting for transfers between devices, local(): pieces = lax.all_to_all(pair, 'exp', 0, 0, axis_index_groups=same_core)  21.9 us
    all_to_all x1, starting transfers between devices, local(): pieces = lax.all_to_all(pair, 'exp', 0, 0, axis_index_groups=same_core)  15.2 us
    pallas_call x13, Pallas kernels, run_kernel(): pl.pallas_call(body, out_shape=[jax.ShapeDtypeStruct(shape, dtype) for sh...  13.8 us
  transfers between devices with their start and end apart: 4, of which 4 were waited for; matrix products, arithmetic and copies ran while one was open for 0% of the time, Pallas kernels for 1%

profile of v4, /device:TPU:32, one launch (start us, length us, event | category | flops | bytes accessed | tf_op | source)
XLA Modules:
  0.0 245.6 jit_solution(11363562688175853072)
XLA Ops:
  2.8 1.3 shard_map.146
  4.1 7.0 %all-to-all-start = ((bf16[16,144,128]{2,1,0:T(8,128)(2,1)}), bf16[16,144,128]{2,1,0:T(8,128)(2,1)S(1)}, u32[]{:S(2)}, u32[]{:S(2)}) async-start(bf16[16,144,128]{2,1,0:T(8,128)(2,1)} %shard_map.146), calls=%async_computation | async-start | bytes 1179648 | tf_op jit(solution)/shard_map/all_to_all | solution.py:315
  11.2 1.1 copy-done
  15.9 7.2 %all-to-all-done.arrived.tails = bf16[16,144,128]{2,1,0:T(8,128)(2,1)S(1)} async-done(((bf16[16,144,128]{2,1,0:T(8,128)(2,1)}), bf16[16,144,128]{2,1,0:T(8,128)(2,1)S(1)}, u32[]{:S(2)}, u32[]{:S(2)}) %all-to-all-start) | async-done | bytes 589856 | tf_op jit(solution)/shard_map/all_to_all | solution.py:315
  23.1 1.3 shard_map.148
  24.4 1.9 collective-permute-start
  26.3 1.7 collective-permute-done
  28.0 0.8 add_convert_fusion
  28.9 15.2 %all-to-all-start.1 = ((bf16[16,96,128]{2,1,0:T(8,128)(2,1)}), bf16[16,96,128]{2,1,0:T(8,128)(2,1)S(1)}, u32[]{:S(2)}, u32[]{:S(2)}) async-start(bf16[16,96,128]{2,1,0:T(8,128)(2,1)} %add_convert_fusion), calls=%async_computation.1 | async-start | bytes 786432 | tf_op jit(solution)/shard_map/all_to_all | solution.py:337
  44.3 21.9 %all-to-all-done.1.pieces = bf16[16,96,128]{2,1,0:T(8,128)(2,1)S(1)} async-done(((bf16[16,96,128]{2,1,0:T(8,128)(2,1)}), bf16[16,96,128]{2,1,0:T(8,128)(2,1)S(1)}, u32[]{:S(2)}, u32[]{:S(2)}) %all-to-all-start.1) | async-done | bytes 393248 | tf_op jit(solution)/shard_map/all_to_all | solution.py:337
  66.7 26.2 %all_to_all.45.rows = bf16[32,24,128]{2,1,0:T(8,128)(2,1)S(1)} all-to-all(bf16[32,24,128]{2,1,0:T(8,128)(2,1)S(1)} %get-tuple-element.38), channel_id=1, replica_groups=mesh['ctx'=16,'exp'=32] {'exp'}, dimensions={0} | all-to-all | bytes 393216 | tf_op jit(solution)/shard_map/all_to_all | solution.py:344
  93.1 12.0 %all_to_all.46 = bf16[4,32,3072]{2,1,0:T(8,128)(2,1)S(1)} all-to-all(bf16[4,32,3072]{2,1,0:T(8,128)(2,1)S(1)} %get-tuple-element.39), channel_id=1, replica_groups={{0,32,64,96},{128,160,192,224},{256,288,320,352},{384,416,448,480},{1,1..., dimensions={0} | all-to-all | bytes 1572864 | tf_op jit(solution)/shard_map/all_to_all | solution.py:350
  105.5 25.0 %all_to_all.47 = bf16[4,128,3072]{2,1,0:T(8,128)(2,1)S(1)} all-to-all(bf16[4,128,3072]{2,1,0:T(8,128)(2,1)S(1)} %broadcast_in_dim.8), channel_id=1, replica_groups={{0,128,256,384},{32,160,288,416},{64,192,320,448},{96,224,352,480},{1,3..., dimensions={0} | all-to-all | bytes 6291456 | tf_op jit(solution)/shard_map/all_to_all | solution.py:352
  130.5 3.4 %shard_map.152 = bf16[16,32,3072]{2,1,0:T(8,128)(2,1)S(1)} custom-call(bf16[3072,384]{1,0:T(8,128)(2,1)S(1)} %bitcast.15, bf16[384,3072]{1,0:T(8,128)(2,1)S(1)} %bitcast.16, bf16[16,32,3072]{2,1,0:T(8,128)(2,1)S(1)} %bitcast.13), custom_call_target="tpu_custom_call" | custom-call | flops 2400000000 | bytes 11000000 | tf_op jit(solution)/shard_map/pallas_call | solution.py:43
  134.0 24.6 %all_to_all.48.sums = bf16[4,128,3072]{2,1,0:T(8,128)(2,1)S(1)} all-to-all(bf16[4,128,3072]{2,1,0:T(8,128)(2,1)S(1)} %bitcast.14), channel_id=1, replica_groups={{0,128,256,384},{32,160,288,416},{64,192,320,448},{96,224,352,480},{1,3..., dimensions={0} | all-to-all | bytes 6291456 | tf_op jit(solution)/shard_map/all_to_all | solution.py:362
  159.1 12.0 %all_to_all.49.sums = bf16[4,32,3072]{2,1,0:T(8,128)(2,1)S(1)} all-to-all(bf16[4,32,3072]{2,1,0:T(8,128)(2,1)S(1)} %shard_map.153), channel_id=1, replica_groups={{0,32,64,96},{128,160,192,224},{256,288,320,352},{384,416,448,480},{1,1..., dimensions={0} | all-to-all | bytes 1572864 | tf_op jit(solution)/shard_map/all_to_all | solution.py:366
  171.7 23.1 %all_to_all.50.returned = bf16[32,24,128]{2,1,0:T(8,128)(2,1)S(1)} all-to-all(bf16[32,24,128]{2,1,0:T(8,128)(2,1)S(1)} %shard_map.154), channel_id=1, replica_groups=mesh['ctx'=16,'exp'=32] {'exp'}, dimensions={0} | all-to-all | bytes 393216 | tf_op jit(solution)/shard_map/all_to_all | solution.py:368
  194.8 1.0 shard_map.155
  195.8 30.9 %all_gather.3.turned_grads = bf16[3072,128]{1,0:T(8,128)(2,1)S(1)} all-gather(bf16[96,128]{1,0:T(8,128)(2,1)} %get-tuple-element.44), channel_id=1, replica_groups=mesh['ctx'=16,'exp'=32] {'exp'}, dimensions={0}, use_global_device_ids=true | all-gather | bytes 811008 | tf_op jit(solution)/shard_map/all_gather | solution.py:374
  226.7 1.5 shard_map.156
  228.2 3.6 %all-to-all-start.8 = ((bf16[16,128,128]{2,1,0:T(8,128)(2,1)}), bf16[16,128,128]{2,1,0:T(8,128)(2,1)S(1)}, u32[]{:S(2)}, u32[]{:S(2)}) async-start(bf16[16,128,128]{2,1,0:T(8,128)(2,1)} %get-tuple-element.51), calls=%async_computation.8 | async-start | bytes 1048576 | tf_op jit(solution)/shard_map/all_to_all | solution.py:380
  231.8 1.2 shard_map.157
  233.0 11.0 %all-to-all-done.8.arrived = bf16[16,128,128]{2,1,0:T(8,128)(2,1)S(1)} async-done(((bf16[16,128,128]{2,1,0:T(8,128)(2,1)}), bf16[16,128,128]{2,1,0:T(8,128)(2,1)S(1)}, u32[]{:S(2)}, u32[]{:S(2)}) %all-to-all-start.8) | async-done | bytes 524320 | tf_op jit(solution)/shard_map/all_to_all | solution.py:380
  244.0 1.6 shard_map.158
  (43 shorter events, 8.1 us)
Async XLA Ops:
  0.6 0.8 copy-start.4
  1.4 0.8 copy-start.7
  2.2 0.7 copy-start.14
  2.8 41.3 %copy-start.13 = (bf16[128,96]{0,1:T(8,128)(2,1)S(1)}, bf16[128,96]{0,1:T(8,128)(2,1)}, u32[]{:S(2)}) copy-start(bf16[128,96]{0,1:T(8,128)(2,1)} %param.21) | copy-start | bytes 73732
  2.8 41.3 %copy-start.16 = (f32[128,2]{0,1:T(2,128)S(1)}, f32[128,2]{0,1:T(2,128)}, u32[]{:S(2)}) copy-start(f32[128,2]{0,1:T(2,128)} %param.20) | copy-start | bytes 3076
  2.8 41.3 %copy-start.17 = (s32[128,2]{0,1:T(2,128)S(1)}, s32[128,2]{0,1:T(2,128)}, u32[]{:S(2)}) copy-start(s32[128,2]{0,1:T(2,128)} %param.19) | copy-start | bytes 3076
  2.8 63.4 %copy-start.12 = (bf16[128,96]{0,1:T(8,128)(2,1)S(1)}, bf16[128,96]{0,1:T(8,128)(2,1)}, u32[]{:S(2)}) copy-start(bf16[128,96]{0,1:T(8,128)(2,1)} %param.11) | copy-start | bytes 73732
  4.1 19.0 %all-to-all-start = ((bf16[16,144,128]{2,1,0:T(8,128)(2,1)}), bf16[16,144,128]{2,1,0:T(8,128)(2,1)S(1)}, u32[]{:S(2)}, u32[]{:S(2)}) async-start(bf16[16,144,128]{2,1,0:T(8,128)(2,1)} %shard_map.146), calls=%async_computation | async-start | bytes 1179648 | tf_op jit(solution)/shard_map/all_to_all | solution.py:315
  11.2 1.1 copy-start
  12.3 0.8 copy-start.5
  13.1 0.8 copy-start.8
  13.8 0.8 copy-start.10
  14.6 0.7 copy-start.15
  24.4 3.6 %collective-permute-start = (bf16[16,96,128]{2,1,0:T(8,128)(2,1)S(1)}, bf16[16,96,128]{2,1,0:T(8,128)(2,1)S(1)}, u32[]{:S(2)}, u32[]{:S(2)}) collective-permute-start(bf16[16,96,128]{2,1,0:T(8,128)(2,1)S(1)} %get-tuple-element.35), channel_id=1, source_target_pairs={{0,1},{1,0},{2,3},{3,2},{4,5},{5,4},{6,7},{7,6},{8,9},{9,8},{10,11... | collective-permute-start | bytes 1179656 | tf_op jit(solution)/shard_map/ppermute | solution.py:335
  28.9 37.4 %all-to-all-start.1 = ((bf16[16,96,128]{2,1,0:T(8,128)(2,1)}), bf16[16,96,128]{2,1,0:T(8,128)(2,1)S(1)}, u32[]{:S(2)}, u32[]{:S(2)}) async-start(bf16[16,96,128]{2,1,0:T(8,128)(2,1)} %add_convert_fusion), calls=%async_computation.1 | async-start | bytes 786432 | tf_op jit(solution)/shard_map/all_to_all | solution.py:337
  105.5 25.0 %copy-start.2 = (bf16[1,3072,384]{2,1,0:T(8,128)(2,1)S(1)}, bf16[1,3072,384]{2,1,0:T(8,128)(2,1)}, u32[]{:S(2)}) copy-start(bf16[1,3072,384]{2,1,0:T(8,128)(2,1)} %param.17) | copy-start | bytes 7077892
  105.5 25.0 %copy-start.3 = (bf16[1,384,3072]{2,1,0:T(8,128)(2,1)S(1)}, bf16[1,384,3072]{2,1,0:T(8,128)(2,1)}, u32[]{:S(2)}) copy-start(bf16[1,384,3072]{2,1,0:T(8,128)(2,1)} %param.18) | copy-start | bytes 7077892
  159.1 67.6 %copy-start.1 = (bf16[128,3072]{1,0:T(8,128)(2,1)S(1)}, bf16[128,3072]{1,0:T(8,128)(2,1)}, u32[]{:S(2)}) copy-start(bf16[128,3072]{1,0:T(8,128)(2,1)} %w_out.3) | copy-start | bytes 2359300
  171.2 60.6 %copy-start.6 = (bf16[128,128]{1,0:T(8,128)(2,1)S(1)}, bf16[128,128]{1,0:T(8,128)(2,1)}, u32[]{:S(2)}) copy-start(bf16[128,128]{1,0:T(8,128)(2,1)} %keys.5) | copy-start | bytes 98308
  171.2 60.6 %copy-start.9 = (bf16[128,128]{1,0:T(8,128)(2,1)S(1)}, bf16[128,128]{1,0:T(8,128)(2,1)}, u32[]{:S(2)}) copy-start(bf16[128,128]{1,0:T(8,128)(2,1)} %values.5) | copy-start | bytes 98308
  171.2 60.6 %copy-start.11 = (bf16[128,128]{1,0:T(8,128)(2,1)S(1)}, bf16[128,128]{1,0:T(8,128)(2,1)}, u32[]{:S(2)}) copy-start(bf16[128,128]{1,0:T(8,128)(2,1)} %queries.3) | copy-start | bytes 98308
  228.2 15.8 %all-to-all-start.8 = ((bf16[16,128,128]{2,1,0:T(8,128)(2,1)}), bf16[16,128,128]{2,1,0:T(8,128)(2,1)S(1)}, u32[]{:S(2)}, u32[]{:S(2)}) async-start(bf16[16,128,128]{2,1,0:T(8,128)(2,1)} %get-tuple-element.51), calls=%async_computation.8 | async-start | bytes 1048576 | tf_op jit(solution)/shard_map/all_to_all | solution.py:380

commit v5 on v4

--- a/solution.py
+++ b/solution.py
@@ -97,22 +97,28 @@
         packed[block, dh:, :] = tail.astype(bf16)
 
 
-def inner_kernel(queries, keys, values, log_decay, w_out, scores, inner, decay, grow, keep, grown, w_turned):
+def inner_kernel(
+    place, log_decay, w_out, heads_in, scores, inner, decay, grow, keep, grown, mine, theirs
+):
     cum = running(log_decay[...])
     n = cum.shape[0]
     causal = iota((n, n), 0) >= iota((n, n), 1)
     gaps = jnp.where(causal, cum - turned(cum), 0.0)
     fall = jnp.where(causal, jnp.exp(gaps), 0.0)
-    pairs = mm_high(queries[...].astype(f32), keys[...].astype(f32), ((1,), (1,))) * fall
+    pairs = mm_high(heads_in[0].astype(f32), heads_in[1].astype(f32), ((1,), (1,))) * fall
     scores[...] = pairs
     decay[...] = fall
-    inner[...] = mm_high(pairs, values[...].astype(f32), ((1,), (0,)))
+    inner[...] = mm_high(pairs, heads_in[2].astype(f32), ((1,), (0,)))
     grow[...] = jnp.broadcast_to(jnp.exp(cum), grow.shape)
-    grown[...] = queries[...].astype(f32) * jnp.exp(cum)
+    grown[...] = heads_in[0].astype(f32) * jnp.exp(cum)
     keep[...] = jnp.broadcast_to(jnp.exp(cum[n - 1 :, :] - cum), keep.shape)
-    dh = w_out.shape[0]
-    for start in range(0, w_out.shape[1], dh):
-        w_turned[start : start + dh, :] = w_out[:, start : start + dh].astype(f32).T.astype(bf16)
+    dh, width = w_out.shape
+    chips, share, _ = mine.shape
+    blocks = [w_out[:, at : at + dh].astype(f32).T.astype(bf16) for at in range(0, width, dh)]
+    flipped = jnp.concatenate(blocks, axis=0).reshape(chips, 2, share, dh)
+    even = lax.rem(place[1], 2) == 0
+    mine[...] = jnp.where(even, flipped[:, 0], flipped[:, 1])
+    theirs[...] = jnp.where(even, flipped[:, 1], flipped[:, 0])
 
 
 def route_kernel(ids, weights, cotangent, picks, cot_parts, *, cap):
@@ -132,8 +138,8 @@
         cot_parts[:, at] = (weights[j : j + 1, :] * cot).astype(bf16)
 
 
-def heads_kernel(place, arrived, inner, grown, w_turned, mine, other, incoming):
-    me, core = place[0], lax.rem(place[1], 2)
+def heads_kernel(place, arrived, inner, grown, heads, incoming):
+    me = place[0]
     blocks = arrived.shape[0]
     dh = grown.shape[1]
     total = jnp.zeros((dh, dh), f32)
@@ -144,12 +150,14 @@
         last = jnp.sum(arrived[block, dh:, :].astype(f32), axis=0, keepdims=True)
         gap = gap + jnp.where(block < me, last, 0.0)
     incoming[...] = total
-    heads = (inner[...] + mm_high(grown[...], total, ((1,), (0,)))).astype(bf16)
-    chips, share, _ = mine.shape
-    partial = mm(w_turned[...], heads, ((1,), (1,))).astype(bf16)
-    partial = partial.reshape(chips, 2, share, heads.shape[0])
-    mine[...] = jnp.where(core == 0, partial[:, 0], partial[:, 1])
-    other[...] = jnp.where(core == 0, partial[:, 1], partial[:, 0])
+    heads[...] = (inner[...] + mm_high(grown[...], total, ((1,), (0,)))).astype(bf16)
+
+
+def project_kernel(heads, heads_given, weights, weights_given, partial):
+    chips, share, dh = weights.shape
+    both = jnp.concatenate([weights[...], weights_given[...]], axis=2).reshape(chips * share, 2 * dh)
+    pair = jnp.concatenate([heads[...], heads_given[...]], axis=1)
+    partial[...] = mm(both, pair, ((1,), (1,))).astype(bf16).reshape(partial.shape)
 
 
 def send_kernel(resid, pieces, cot_parts, picks, residual, sent):
@@ -232,13 +240,12 @@
     share, tokens = residual.shape
     slots_all = picks.shape[0]
     left, right = unpack(returned[...].astype(f32), share)
-    left = left.reshape(slots_all, share).astype(bf16)
-    right = right.reshape(slots_all, share).astype(bf16)
-    both = mm(left, picks[...], ((0,), (0,)))
+    rows = jnp.concatenate([left, right], axis=2).reshape(slots_all, 2 * share).astype(bf16)
+    all_rows = mm(rows, picks[...], ((0,), (0,)))
+    both = all_rows[:share]
     routed = weights[0:1, :] * both[:, :tokens] + weights[1:2, :] * both[:, tokens:]
     layer_out[...] = (residual[...].astype(f32) + routed).astype(bf16)
-    placed = picks[:, :tokens] + picks[:, tokens:]
-    summed = mm(right, placed, ((0,), (0,)))
+    summed = all_rows[share:, :tokens] + all_rows[share:, tokens:]
     resid_grad[...] = (cotangent[...].astype(f32) + summed).astype(bf16)
 
 
@@ -252,18 +259,18 @@
 
 
 def grads_kernel(
-    queries, keys, values, grad_heads, scores, decay, grow, incoming, q_grad, k_part, v_part
+    heads_in, grad_heads, scores, decay, grow, incoming, q_grad, k_part, v_part
 ):
     grads = grad_heads[...]
-    score_grad = mm_high(grads, values[...].astype(f32), ((1,), (1,))) * decay[...]
-    direct = mm_high(score_grad, keys[...].astype(f32), ((1,), (0,)))
+    score_grad = mm_high(grads, heads_in[2].astype(f32), ((1,), (1,))) * decay[...]
+    direct = mm_high(score_grad, heads_in[1].astype(f32), ((1,), (0,)))
     carried = mm_high(grads, incoming[...], ((1,), (1,)))
     q_grad[...] = (direct + grow[...] * carried).astype(bf16)
-    k_part[...] = mm_high(score_grad, queries[...].astype(f32), ((0,), (0,)))
+    k_part[...] = mm_high(score_grad, heads_in[0].astype(f32), ((0,), (0,)))
     v_part[...] = mm_high(scores[...], grads, ((0,), (0,)))
 
 
-def last_kernel(place, keys, values, arrived, tails, keep, k_part, v_part, k_grad, v_grad):
+def last_kernel(place, heads_in, arrived, tails, keep, k_part, v_part, k_grad, v_grad):
     me = place[0]
     blocks, dh, _ = arrived.shape
     total = jnp.zeros((dh, dh), f32)
@@ -273,8 +280,8 @@
         total = total + weight * arrived[block].astype(f32)
         last = jnp.sum(tails[block, dh:, :].astype(f32), axis=0, keepdims=True)
         gap = gap + jnp.where(block > me, last, 0.0)
-    from_values = mm_high(values[...].astype(f32), total, ((1,), (1,)))
-    from_keys = mm_high(keys[...].astype(f32), total, ((1,), (0,)))
+    from_values = mm_high(heads_in[2].astype(f32), total, ((1,), (1,)))
+    from_keys = mm_high(heads_in[1].astype(f32), total, ((1,), (0,)))
     k_grad[...] = (k_part[...] + keep[...] * from_values).astype(bf16)
     v_grad[...] = (v_part[...] + keep[...] * from_keys).astype(bf16)
 
@@ -302,6 +309,7 @@
     square = (tokens, dh)
     flat = (share, tokens)
     weights, cot = route_weights.T, cotangent.T
+    heads_in = jnp.stack([queries, keys, values])
     packed_rows = (n_exp, cap * 2 * share // 128, 128)
 
     [packed] = run_kernel(
@@ -311,29 +319,37 @@
         far=3,
         scratch=[pltpu.VMEM(square, bf16)] * 2
         + [pltpu.VMEM(log_decay.shape, f32), pltpu.SemaphoreType.DMA((3,))],
+        limit=56,
     )
     arrived = lax.all_to_all(packed, "ctx", 0, 0)
-    scores, inner, decay, grow, keep, grown, w_turned = run_kernel(
+    scores, inner, decay, grow, keep, grown, w_mine, w_theirs = run_kernel(
         inner_kernel,
         [((tokens, tokens), f32), (square, f32), ((tokens, tokens), f32), (square, f32), (square, f32)]
-        + [(square, f32), ((width, dh), bf16)],
-        (queries, keys, values, log_decay, w_out),
-        raw=5,
-    )
+        + [(square, f32)]
+        + [((chips, share, dh), bf16)] * 2,
+        (place, log_decay, w_out, heads_in),
+        smem=1,
+        raw=2,
+    )
+    w_given = lax.ppermute(w_theirs, "exp", partner)
     picks, cot_parts = run_kernel(
         functools.partial(route_kernel, cap=cap),
         [((n_exp * cap, 2 * tokens), bf16), ((share, 2 * tokens), bf16)],
         (expert_ids.T, weights, cot),
         raw=3,
     )
-    mine, other, incoming = run_kernel(
+    heads, incoming = run_kernel(
         heads_kernel,
-        [((chips, share, tokens), bf16)] * 2 + [((dh, dh), f32)],
-        (place, arrived, inner, grown, w_turned),
+        [((tokens, dh), bf16), ((dh, dh), f32)],
+        (place, arrived, inner, grown),
         smem=1,
     )
-    other = lax.ppermute(other, "exp", partner)
-    pair = (mine.astype(f32) + other.astype(f32)).astype(bf16)
+    heads_given = lax.ppermute(heads, "exp", partner)
+    [pair] = run_kernel(
+        project_kernel,
+        [((chips, share, tokens), bf16)],
+        (heads, heads_given, w_mine, w_given),
+    )
     pieces = lax.all_to_all(pair, "exp", 0, 0, axis_index_groups=same_core)
     residual, sent = run_kernel(
         send_kernel,
@@ -352,7 +368,7 @@
     everyone = lax.all_to_all(line, axes, 0, 0, axis_index_groups=second)
     everyone = everyone.reshape(n_ctx, 2 * cap, width)
     [sums] = run_kernel(
-        functools.partial(expert_kernel, step=512 if width % 512 == 0 else 384),
+        functools.partial(expert_kernel, step=1024 if width % 1024 == 0 else 384),
         [((n_ctx, 2 * cap, width), bf16)],
         (w_up[0], w_down[0], everyone),
         flops=2_400_000_000,
@@ -381,12 +397,12 @@
     q_grad, k_part, v_part = run_kernel(
         grads_kernel,
         [(square, bf16), (square, f32), (square, f32)],
-        (queries, keys, values, grad_heads, scores, decay, grow, incoming),
+        (heads_in, grad_heads, scores, decay, grow, incoming),
     )
     k_grad, v_grad = run_kernel(
         last_kernel,
         [(square, bf16), (square, bf16)],
-        (place, keys, values, states, arrived, keep, k_part, v_part),
+        (place, heads_in, states, arrived, keep, k_part, v_part),
         smem=1,
     )
     return layer_out.T, resid_grad.T, q_grad, k_grad, v_grad

time: 247 us -> 244 us (0.988)
  local copies, waits for them, and re-layouts: 6.63 us -> 2.19 us
    unnamed x36 -> x18, local copies, waits for them, and re-layouts: 6.27 us -> 1.82 us
    pallas_call x13 -> x14, Pallas kernels: 13.8 us -> 15.7 us  [run_kernel(): pl.pallas_call(body, out_shape=[jax.ShapeDtypeStruct(shape, dtype) for sh...]
  transfers between devices with their start and end apart: 4 -> 5, of which waited for: 4 -> 4; matrix products, arithmetic and copies ran while one was open for 0% -> 0% of each run, Pallas kernels for 1% -> 1%
where the time goes in v5:
time: 244 us; the launch traced here: 243 us
  blocking collectives  154 us (63%)
  waiting for transfers between devices  40.4 us (17%)
  starting transfers between devices  29.7 us (12%)
  Pallas kernels  15.7 us (6%)
    all_gather x1, blocking collectives, local(): turned_grads = lax.all_gather(resid_grad, 'exp', tiled=True)  30.9 us
    all_to_all x1, blocking collectives, local(): rows = lax.all_to_all(sent, 'exp', 0, 0)  26.2 us
    all_to_all x1, blocking collectives, local(): everyone = lax.all_to_all(line, axes, 0, 0, axis_index_groups=second)  25 us
    all_to_all x1, blocking collectives, local(): sums = lax.all_to_all(sums, axes, 0, 0, axis_index_groups=second)  24.6 us
    all_to_all x1, blocking collectives, local(): returned = lax.all_to_all(returned, 'exp', 0, 0)  23.1 us
    all_to_all x1, waiting for transfers between devices, local(): pieces = lax.all_to_all(pair, 'exp', 0, 0, axis_index_groups=same_core)  22 us
    pallas_call x14, Pallas kernels, run_kernel(): pl.pallas_call(body, out_shape=[jax.ShapeDtypeStruct(shape, dtype) for sh...  15.7 us
    all_to_all x1, starting transfers between devices, local(): pieces = lax.all_to_all(pair, 'exp', 0, 0, axis_index_groups=same_core)  15.2 us
  transfers between devices with their start and end apart: 5, of which 4 were waited for; matrix products, arithmetic and copies ran while one was open for 0% of the time, Pallas kernels for 1%

profile of v5, /device:TPU:32, one launch (start us, length us, event | category | flops | bytes accessed | tf_op | source)
XLA Modules:
  0.0 243.4 jit_solution(8974941046392124560)
XLA Ops:
  0.7 2.0 shard_map.146
  2.7 7.0 %all-to-all-start = ((bf16[16,144,128]{2,1,0:T(8,128)(2,1)}), bf16[16,144,128]{2,1,0:T(8,128)(2,1)S(1)}, u32[]{:S(2)}, u32[]{:S(2)}) async-start(bf16[16,144,128]{2,1,0:T(8,128)(2,1)} %shard_map.146), calls=%async_computation | async-start | bytes 1179648 | tf_op jit(solution)/shard_map/all_to_all | solution.py:324
  10.7 1.1 copy-done
  12.4 1.1 shard_map.147
  13.5 1.9 collective-permute-start.1
  15.4 6.2 %all-to-all-done.arrived.tails = bf16[16,144,128]{2,1,0:T(8,128)(2,1)S(1)} async-done(((bf16[16,144,128]{2,1,0:T(8,128)(2,1)}), bf16[16,144,128]{2,1,0:T(8,128)(2,1)S(1)}, u32[]{:S(2)}, u32[]{:S(2)}) %all-to-all-start) | async-done | bytes 589856 | tf_op jit(solution)/shard_map/all_to_all | solution.py:324
  22.5 1.9 collective-permute-start
  24.5 1.2 collective-permute-done.heads_given
  25.6 1.1 shard_map.149
  26.8 15.2 %all-to-all-start.1 = ((bf16[16,96,128]{2,1,0:T(8,128)(2,1)}), bf16[16,96,128]{2,1,0:T(8,128)(2,1)S(1)}, u32[]{:S(2)}, u32[]{:S(2)}) async-start(bf16[16,96,128]{2,1,0:T(8,128)(2,1)} %shard_map.149), calls=%async_computation.1 | async-start | bytes 786432 | tf_op jit(solution)/shard_map/all_to_all | solution.py:353
  42.2 22.0 %all-to-all-done.1.pieces = bf16[16,96,128]{2,1,0:T(8,128)(2,1)S(1)} async-done(((bf16[16,96,128]{2,1,0:T(8,128)(2,1)}), bf16[16,96,128]{2,1,0:T(8,128)(2,1)S(1)}, u32[]{:S(2)}, u32[]{:S(2)}) %all-to-all-start.1) | async-done | bytes 393248 | tf_op jit(solution)/shard_map/all_to_all | solution.py:353
  64.6 26.2 %all_to_all.45.rows = bf16[32,24,128]{2,1,0:T(8,128)(2,1)S(1)} all-to-all(bf16[32,24,128]{2,1,0:T(8,128)(2,1)S(1)} %get-tuple-element.38), channel_id=1, replica_groups=mesh['ctx'=16,'exp'=32] {'exp'}, dimensions={0} | all-to-all | bytes 393216 | tf_op jit(solution)/shard_map/all_to_all | solution.py:360
  91.0 12.0 %all_to_all.46 = bf16[4,32,3072]{2,1,0:T(8,128)(2,1)S(1)} all-to-all(bf16[4,32,3072]{2,1,0:T(8,128)(2,1)S(1)} %get-tuple-element.39), channel_id=1, replica_groups={{0,32,64,96},{128,160,192,224},{256,288,320,352},{384,416,448,480},{1,1..., dimensions={0} | all-to-all | bytes 1572864 | tf_op jit(solution)/shard_map/all_to_all | solution.py:366
  103.5 25.0 %all_to_all.47 = bf16[4,128,3072]{2,1,0:T(8,128)(2,1)S(1)} all-to-all(bf16[4,128,3072]{2,1,0:T(8,128)(2,1)S(1)} %broadcast_in_dim.8), channel_id=1, replica_groups={{0,128,256,384},{32,160,288,416},{64,192,320,448},{96,224,352,480},{1,3..., dimensions={0} | all-to-all | bytes 6291456 | tf_op jit(solution)/shard_map/all_to_all | solution.py:368
  128.4 3.5 %shard_map.153 = bf16[16,32,3072]{2,1,0:T(8,128)(2,1)S(1)} custom-call(bf16[3072,384]{1,0:T(8,128)(2,1)S(1)} %bitcast.18, bf16[384,3072]{1,0:T(8,128)(2,1)S(1)} %bitcast.19, bf16[16,32,3072]{2,1,0:T(8,128)(2,1)S(1)} %bitcast.16), custom_call_target="tpu_custom_call" | custom-call | flops 2400000000 | bytes 11000000 | tf_op jit(solution)/shard_map/pallas_call | solution.py:43
  131.9 24.6 %all_to_all.48.sums = bf16[4,128,3072]{2,1,0:T(8,128)(2,1)S(1)} all-to-all(bf16[4,128,3072]{2,1,0:T(8,128)(2,1)S(1)} %bitcast.17), channel_id=1, replica_groups={{0,128,256,384},{32,160,288,416},{64,192,320,448},{96,224,352,480},{1,3..., dimensions={0} | all-to-all | bytes 6291456 | tf_op jit(solution)/shard_map/all_to_all | solution.py:378
  157.1 12.0 %all_to_all.49.sums = bf16[4,32,3072]{2,1,0:T(8,128)(2,1)S(1)} all-to-all(bf16[4,32,3072]{2,1,0:T(8,128)(2,1)S(1)} %shard_map.154), channel_id=1, replica_groups={{0,32,64,96},{128,160,192,224},{256,288,320,352},{384,416,448,480},{1,1..., dimensions={0} | all-to-all | bytes 1572864 | tf_op jit(solution)/shard_map/all_to_all | solution.py:382
  169.6 23.1 %all_to_all.50.returned = bf16[32,24,128]{2,1,0:T(8,128)(2,1)S(1)} all-to-all(bf16[32,24,128]{2,1,0:T(8,128)(2,1)S(1)} %shard_map.155), channel_id=1, replica_groups=mesh['ctx'=16,'exp'=32] {'exp'}, dimensions={0} | all-to-all | bytes 393216 | tf_op jit(solution)/shard_map/all_to_all | solution.py:384
  193.6 30.9 %all_gather.3.turned_grads = bf16[3072,128]{1,0:T(8,128)(2,1)S(1)} all-gather(bf16[96,128]{1,0:T(8,128)(2,1)} %get-tuple-element.44), channel_id=1, replica_groups=mesh['ctx'=16,'exp'=32] {'exp'}, dimensions={0}, use_global_device_ids=true | all-gather | bytes 811008 | tf_op jit(solution)/shard_map/all_gather | solution.py:390
  224.5 1.5 shard_map.157
  226.0 3.6 %all-to-all-start.8 = ((bf16[16,128,128]{2,1,0:T(8,128)(2,1)}), bf16[16,128,128]{2,1,0:T(8,128)(2,1)S(1)}, u32[]{:S(2)}, u32[]{:S(2)}) async-start(bf16[16,128,128]{2,1,0:T(8,128)(2,1)} %get-tuple-element.51), calls=%async_computation.8 | async-start | bytes 1048576 | tf_op jit(solution)/shard_map/all_to_all | solution.py:396
  229.6 1.2 shard_map.158
  230.8 11.1 %all-to-all-done.8.arrived = bf16[16,128,128]{2,1,0:T(8,128)(2,1)S(1)} async-done(((bf16[16,128,128]{2,1,0:T(8,128)(2,1)}), bf16[16,128,128]{2,1,0:T(8,128)(2,1)S(1)}, u32[]{:S(2)}, u32[]{:S(2)}) %all-to-all-start.8) | async-done | bytes 524320 | tf_op jit(solution)/shard_map/all_to_all | solution.py:396
  241.8 1.6 shard_map.159
  (28 shorter events, 5.7 us)
Async XLA Ops:
  0.6 41.3 %copy-start.5 = (bf16[128,96]{0,1:T(8,128)(2,1)S(1)}, bf16[128,96]{0,1:T(8,128)(2,1)}, u32[]{:S(2)}) copy-start(bf16[128,96]{0,1:T(8,128)(2,1)} %param.21) | copy-start | bytes 73732
  0.6 41.3 %copy-start.7 = (f32[128,2]{0,1:T(2,128)S(1)}, f32[128,2]{0,1:T(2,128)}, u32[]{:S(2)}) copy-start(f32[128,2]{0,1:T(2,128)} %param.20) | copy-start | bytes 3076
  0.7 41.3 %copy-start.8 = (s32[128,2]{0,1:T(2,128)S(1)}, s32[128,2]{0,1:T(2,128)}, u32[]{:S(2)}) copy-start(s32[128,2]{0,1:T(2,128)} %param.19) | copy-start | bytes 3076
  0.7 63.5 %copy-start.4 = (bf16[128,96]{0,1:T(8,128)(2,1)S(1)}, bf16[128,96]{0,1:T(8,128)(2,1)}, u32[]{:S(2)}) copy-start(bf16[128,96]{0,1:T(8,128)(2,1)} %param.11) | copy-start | bytes 73732
  2.7 19.0 %all-to-all-start = ((bf16[16,144,128]{2,1,0:T(8,128)(2,1)}), bf16[16,144,128]{2,1,0:T(8,128)(2,1)S(1)}, u32[]{:S(2)}, u32[]{:S(2)}) async-start(bf16[16,144,128]{2,1,0:T(8,128)(2,1)} %shard_map.146), calls=%async_computation | async-start | bytes 1179648 | tf_op jit(solution)/shard_map/all_to_all | solution.py:324
  10.7 1.1 copy-start
  11.8 0.7 copy-start.6
  13.5 11.0 %collective-permute-start.1 = (bf16[16,96,128]{2,1,0:T(8,128)(2,1)S(1)}, bf16[16,96,128]{2,1,0:T(8,128)(2,1)S(1)}, u32[]{:S(2)}, u32[]{:S(2)}) collective-permute-start(bf16[16,96,128]{2,1,0:T(8,128)(2,1)S(1)} %get-tuple-element.35), channel_id=1, source_target_pairs={{0,1},{1,0},{2,3},{3,2},{4,5},{5,4},{6,7},{7,6},{8,9},{9,8},{10,11... | collective-permute-start | bytes 1179656 | tf_op jit(solution)/shard_map/ppermute | solution.py:334
  22.5 3.1 %collective-permute-start = (bf16[128,128]{1,0:T(8,128)(2,1)S(1)}, bf16[128,128]{1,0:T(8,128)(2,1)S(1)}, u32[]{:S(2)}, u32[]{:S(2)}) collective-permute-start(bf16[128,128]{1,0:T(8,128)(2,1)S(1)} %get-tuple-element.33.heads), channel_id=1, source_target_pairs={{0,1},{1,0},{2,3},{3,2},{4,5},{5,4},{6,7},{7,6},{8,9},{9,8},{10,11... | collective-permute-start | bytes 98312 | tf_op jit(solution)/shard_map/ppermute | solution.py:347
  26.8 37.4 %all-to-all-start.1 = ((bf16[16,96,128]{2,1,0:T(8,128)(2,1)}), bf16[16,96,128]{2,1,0:T(8,128)(2,1)S(1)}, u32[]{:S(2)}, u32[]{:S(2)}) async-start(bf16[16,96,128]{2,1,0:T(8,128)(2,1)} %shard_map.149), calls=%async_computation.1 | async-start | bytes 786432 | tf_op jit(solution)/shard_map/all_to_all | solution.py:353
  103.4 25.0 %copy-start.2 = (bf16[1,3072,384]{2,1,0:T(8,128)(2,1)S(1)}, bf16[1,3072,384]{2,1,0:T(8,128)(2,1)}, u32[]{:S(2)}) copy-start(bf16[1,3072,384]{2,1,0:T(8,128)(2,1)} %param.17) | copy-start | bytes 7077892
  103.4 25.0 %copy-start.3 = (bf16[1,384,3072]{2,1,0:T(8,128)(2,1)S(1)}, bf16[1,384,3072]{2,1,0:T(8,128)(2,1)}, u32[]{:S(2)}) copy-start(bf16[1,384,3072]{2,1,0:T(8,128)(2,1)} %param.18) | copy-start | bytes 7077892
  157.1 67.4 %copy-start.1 = (bf16[128,3072]{1,0:T(8,128)(2,1)S(1)}, bf16[128,3072]{1,0:T(8,128)(2,1)}, u32[]{:S(2)}) copy-start(bf16[128,3072]{1,0:T(8,128)(2,1)} %w_out.3) | copy-start | bytes 2359300
  226.0 15.8 %all-to-all-start.8 = ((bf16[16,128,128]{2,1,0:T(8,128)(2,1)}), bf16[16,128,128]{2,1,0:T(8,128)(2,1)S(1)}, u32[]{:S(2)}, u32[]{:S(2)}) async-start(bf16[16,128,128]{2,1,0:T(8,128)(2,1)} %get-tuple-element.51), calls=%async_computation.8 | async-start | bytes 1048576 | tf_op jit(solution)/shard_map/all_to_all | solution.py:396

commit v6 on v5

--- a/solution.py
+++ b/solution.py
@@ -153,7 +153,8 @@
     heads[...] = (inner[...] + mm_high(grown[...], total, ((1,), (0,)))).astype(bf16)
 
 
-def project_kernel(heads, heads_given, weights, weights_given, partial):
+def project_kernel(heads, heads_given, weights, weights_given, picks, partial):
+    del picks
     chips, share, dh = weights.shape
     both = jnp.concatenate([weights[...], weights_given[...]], axis=2).reshape(chips * share, 2 * dh)
     pair = jnp.concatenate([heads[...], heads_given[...]], axis=1)
@@ -233,20 +234,24 @@
     grads = rstd * grads - rows * (rstd * rstd * rstd * inner / width)
     left = jnp.stack([out[:, e * share : (e + 1) * share] for e in range(experts)])
     right = jnp.stack([grads[:, e * share : (e + 1) * share] for e in range(experts)])
-    returned[...] = pack(left, right).astype(bf16)
-
-
-def join_kernel(returned, picks, weights, residual, cotangent, layer_out, resid_grad):
+    returned[...] = pack(right, left).astype(bf16)
+
+
+def resid_grad_kernel(returned, picks, cotangent, resid_grad):
+    share, tokens = cotangent.shape
+    slots_all = picks.shape[0]
+    rows = returned[:, : 2 * returned.shape[1] // 3, :share].reshape(slots_all, share)
+    summed = mm(rows, picks[:, :tokens] + picks[:, tokens:], ((0,), (0,)))
+    resid_grad[...] = (cotangent[...].astype(f32) + summed).astype(bf16)
+
+
+def layer_out_kernel(returned, picks, weights, residual, layer_out):
     share, tokens = residual.shape
     slots_all = picks.shape[0]
-    left, right = unpack(returned[...].astype(f32), share)
-    rows = jnp.concatenate([left, right], axis=2).reshape(slots_all, 2 * share).astype(bf16)
-    all_rows = mm(rows, picks[...], ((0,), (0,)))
-    both = all_rows[:share]
+    _, outs = unpack(returned[...].astype(f32), share)
+    both = mm(outs.reshape(slots_all, share).astype(bf16), picks[...], ((0,), (0,)))
     routed = weights[0:1, :] * both[:, :tokens] + weights[1:2, :] * both[:, tokens:]
     layer_out[...] = (residual[...].astype(f32) + routed).astype(bf16)
-    summed = all_rows[share:, :tokens] + all_rows[share:, tokens:]
-    resid_grad[...] = (cotangent[...].astype(f32) + summed).astype(bf16)
 
 
 def state_grad_kernel(w_out, turned_grads, grown, grad_heads, packed):
@@ -348,7 +353,7 @@
     [pair] = run_kernel(
         project_kernel,
         [((chips, share, tokens), bf16)],
-        (heads, heads_given, w_mine, w_given),
+        (heads, heads_given, w_mine, w_given, picks),
     )
     pieces = lax.all_to_all(pair, "exp", 0, 0, axis_index_groups=same_core)
     residual, sent = run_kernel(
@@ -382,11 +387,7 @@
     sums = lax.all_to_all(sums, axes, 0, 0, axis_index_groups=first)
     [returned] = run_kernel(back_kernel, [(packed_rows, bf16)], (sums, own, rstd))
     returned = lax.all_to_all(returned, "exp", 0, 0)
-    layer_out, resid_grad = run_kernel(
-        join_kernel,
-        [(flat, bf16), (flat, bf16)],
-        (returned, picks, weights, residual, cot),
-    )
+    [resid_grad] = run_kernel(resid_grad_kernel, [(flat, bf16)], (returned, picks, cot))
     turned_grads = lax.all_gather(resid_grad, "exp", tiled=True)
     grad_heads, packed = run_kernel(
         state_grad_kernel,
@@ -398,6 +399,9 @@
         grads_kernel,
         [(square, bf16), (square, f32), (square, f32)],
         (heads_in, grad_heads, scores, decay, grow, incoming),
+    )
+    [layer_out] = run_kernel(
+        layer_out_kernel, [(flat, bf16)], (returned, picks, weights, residual)
     )
     k_grad, v_grad = run_kernel(
         last_kernel,

time: 244 us -> 243 us (level)
  blocking collectives: 154 us -> 191 us
  waiting for transfers between devices: 40.4 us -> 17.2 us
  starting transfers between devices: 29.7 us -> 14.5 us
    all_to_all x0 -> x1, blocking collectives: none -> 37.2 us  [local(): pieces = lax.all_to_all(pair, 'exp', 0, 0, axis_index_groups=same_core)]
    all_to_all x1 -> x0, waiting for transfers between devices: 22 us -> none  [local(): pieces = lax.all_to_all(pair, 'exp', 0, 0, axis_index_groups=same_core)]
    all_to_all x1 -> x0, starting transfers between devices: 15.2 us -> none  [local(): pieces = lax.all_to_all(pair, 'exp', 0, 0, axis_index_groups=same_core)]
    pallas_call x14 -> x15, Pallas kernels: 15.7 us -> 15.7 us  [run_kernel(): pl.pallas_call(body, out_shape=[jax.ShapeDtypeStruct(shape, dtype) for sh...]
  transfers between devices with their start and end apart: 5 -> 4, of which waited for: 4 -> 3; matrix products, arithmetic and copies ran while one was open for 0% -> 0% of each run, Pallas kernels for 1% -> 2%
where the time goes in v6:
time: 243 us; the launch traced here: 242 us
  blocking collectives  191 us (79%)
  waiting for transfers between devices  17.2 us (7%)
  Pallas kernels  15.7 us (6%)
  starting transfers between devices  14.5 us (6%)
    all_to_all x1, blocking collectives, local(): pieces = lax.all_to_all(pair, 'exp', 0, 0, axis_index_groups=same_core)  37.2 us
    all_gather x1, blocking collectives, local(): turned_grads = lax.all_gather(resid_grad, 'exp', tiled=True)  30.9 us
    all_to_all x1, blocking collectives, local(): rows = lax.all_to_all(sent, 'exp', 0, 0)  26.2 us
    all_to_all x1, blocking collectives, local(): everyone = lax.all_to_all(line, axes, 0, 0, axis_index_groups=second)  25 us
    all_to_all x1, blocking collectives, local(): sums = lax.all_to_all(sums, axes, 0, 0, axis_index_groups=second)  24.6 us
    all_to_all x1, blocking collectives, local(): returned = lax.all_to_all(returned, 'exp', 0, 0)  23.1 us
    pallas_call x15, Pallas kernels, run_kernel(): pl.pallas_call(body, out_shape=[jax.ShapeDtypeStruct(shape, dtype) for sh...  15.7 us
    all_to_all x1, blocking collectives, local(): sums = lax.all_to_all(sums, axes, 0, 0, axis_index_groups=first)  12 us
  transfers between devices with their start and end apart: 4, of which 3 were waited for; matrix products, arithmetic and copies ran while one was open for 0% of the time, Pallas kernels for 2%

profile of v6, /device:TPU:32, one launch (start us, length us, event | category | flops | bytes accessed | tf_op | source)
XLA Modules:
  0.0 242.3 jit_solution(2399998596758448971)
XLA Ops:
  0.7 2.0 shard_map.146
  2.7 7.0 %all-to-all-start = ((bf16[16,144,128]{2,1,0:T(8,128)(2,1)}), bf16[16,144,128]{2,1,0:T(8,128)(2,1)S(1)}, u32[]{:S(2)}, u32[]{:S(2)}) async-start(bf16[16,144,128]{2,1,0:T(8,128)(2,1)} %shard_map.146), calls=%async_computation | async-start | bytes 1179648 | tf_op jit(solution)/shard_map/all_to_all | solution.py:329
  10.6 1.1 copy-done
  12.4 1.1 shard_map.147
  13.5 1.9 collective-permute-start.1
  15.4 6.2 %all-to-all-done.arrived.tails = bf16[16,144,128]{2,1,0:T(8,128)(2,1)S(1)} async-done(((bf16[16,144,128]{2,1,0:T(8,128)(2,1)}), bf16[16,144,128]{2,1,0:T(8,128)(2,1)S(1)}, u32[]{:S(2)}, u32[]{:S(2)}) %all-to-all-start) | async-done | bytes 589856 | tf_op jit(solution)/shard_map/all_to_all | solution.py:329
  21.6 0.9 shard_map.148
  22.5 1.9 collective-permute-start
  24.7 0.9 collective-permute-done.heads_given
  26.0 37.2 %all_to_all.45.pieces = bf16[16,96,128]{2,1,0:T(8,128)(2,1)S(1)} all-to-all(bf16[16,96,128]{2,1,0:T(8,128)(2,1)S(1)} %shard_map.150), channel_id=1, replica_groups={{0,2,4,6,8,10,12,14,16,18,20,22,24,26,28,30},{1,3,5,7,9,11,13,15,17,19,..., dimensions={0} | all-to-all | bytes 786432 | tf_op jit(solution)/shard_map/all_to_all | solution.py:358
  63.7 26.2 %all_to_all.46.rows = bf16[32,24,128]{2,1,0:T(8,128)(2,1)S(1)} all-to-all(bf16[32,24,128]{2,1,0:T(8,128)(2,1)S(1)} %get-tuple-element.36), channel_id=1, replica_groups=mesh['ctx'=16,'exp'=32] {'exp'}, dimensions={0} | all-to-all | bytes 393216 | tf_op jit(solution)/shard_map/all_to_all | solution.py:365
  90.1 12.0 %all_to_all.47 = bf16[4,32,3072]{2,1,0:T(8,128)(2,1)S(1)} all-to-all(bf16[4,32,3072]{2,1,0:T(8,128)(2,1)S(1)} %get-tuple-element.37), channel_id=1, replica_groups={{0,32,64,96},{128,160,192,224},{256,288,320,352},{384,416,448,480},{1,1..., dimensions={0} | all-to-all | bytes 1572864 | tf_op jit(solution)/shard_map/all_to_all | solution.py:371
  102.5 25.0 %all_to_all.48 = bf16[4,128,3072]{2,1,0:T(8,128)(2,1)S(1)} all-to-all(bf16[4,128,3072]{2,1,0:T(8,128)(2,1)S(1)} %broadcast_in_dim.8), channel_id=1, replica_groups={{0,128,256,384},{32,160,288,416},{64,192,320,448},{96,224,352,480},{1,3..., dimensions={0} | all-to-all | bytes 6291456 | tf_op jit(solution)/shard_map/all_to_all | solution.py:373
  127.5 3.5 %shard_map.153 = bf16[16,32,3072]{2,1,0:T(8,128)(2,1)S(1)} custom-call(bf16[3072,384]{1,0:T(8,128)(2,1)S(1)} %bitcast.18, bf16[384,3072]{1,0:T(8,128)(2,1)S(1)} %bitcast.19, bf16[16,32,3072]{2,1,0:T(8,128)(2,1)S(1)} %bitcast.16), custom_call_target="tpu_custom_call" | custom-call | flops 2400000000 | bytes 11000000 | tf_op jit(solution)/shard_map/pallas_call | solution.py:43
  130.9 24.6 %all_to_all.49.sums = bf16[4,128,3072]{2,1,0:T(8,128)(2,1)S(1)} all-to-all(bf16[4,128,3072]{2,1,0:T(8,128)(2,1)S(1)} %bitcast.17), channel_id=1, replica_groups={{0,128,256,384},{32,160,288,416},{64,192,320,448},{96,224,352,480},{1,3..., dimensions={0} | all-to-all | bytes 6291456 | tf_op jit(solution)/shard_map/all_to_all | solution.py:383
  156.1 12.0 %all_to_all.50.sums = bf16[4,32,3072]{2,1,0:T(8,128)(2,1)S(1)} all-to-all(bf16[4,32,3072]{2,1,0:T(8,128)(2,1)S(1)} %shard_map.154), channel_id=1, replica_groups={{0,32,64,96},{128,160,192,224},{256,288,320,352},{384,416,448,480},{1,1..., dimensions={0} | all-to-all | bytes 1572864 | tf_op jit(solution)/shard_map/all_to_all | solution.py:387
  168.6 23.1 %all_to_all.51.returned = bf16[32,24,128]{2,1,0:T(8,128)(2,1)S(1)} all-to-all(bf16[32,24,128]{2,1,0:T(8,128)(2,1)S(1)} %shard_map.155), channel_id=1, replica_groups=mesh['ctx'=16,'exp'=32] {'exp'}, dimensions={0} | all-to-all | bytes 393216 | tf_op jit(solution)/shard_map/all_to_all | solution.py:389
  192.4 30.9 %all_gather.3.turned_grads = bf16[3072,128]{1,0:T(8,128)(2,1)S(1)} all-gather(bf16[96,128]{1,0:T(8,128)(2,1)} %shard_map.157), channel_id=1, replica_groups=mesh['ctx'=16,'exp'=32] {'exp'}, dimensions={0}, use_global_device_ids=true | all-gather | bytes 811008 | tf_op jit(solution)/shard_map/all_gather | solution.py:391
  223.4 1.5 shard_map.158
  224.9 3.6 %all-to-all-start.8 = ((bf16[16,128,128]{2,1,0:T(8,128)(2,1)}), bf16[16,128,128]{2,1,0:T(8,128)(2,1)S(1)}, u32[]{:S(2)}, u32[]{:S(2)}) async-start(bf16[16,128,128]{2,1,0:T(8,128)(2,1)} %get-tuple-element.47), calls=%async_computation.8 | async-start | bytes 1048576 | tf_op jit(solution)/shard_map/all_to_all | solution.py:397
  228.5 1.2 shard_map.159
  229.6 1.0 shard_map.156
  230.7 10.1 %all-to-all-done.8.arrived = bf16[16,128,128]{2,1,0:T(8,128)(2,1)S(1)} async-done(((bf16[16,128,128]{2,1,0:T(8,128)(2,1)}), bf16[16,128,128]{2,1,0:T(8,128)(2,1)S(1)}, u32[]{:S(2)}, u32[]{:S(2)}) %all-to-all-start.8) | async-done | bytes 524320 | tf_op jit(solution)/shard_map/all_to_all | solution.py:397
  240.7 1.6 shard_map.160
  (28 shorter events, 5.0 us)
Async XLA Ops:
  0.6 23.8 %copy-start.5 = (bf16[128,96]{0,1:T(8,128)(2,1)S(1)}, bf16[128,96]{0,1:T(8,128)(2,1)}, u32[]{:S(2)}) copy-start(bf16[128,96]{0,1:T(8,128)(2,1)} %param.21) | copy-start | bytes 73732
  0.6 23.8 %copy-start.7 = (f32[128,2]{0,1:T(2,128)S(1)}, f32[128,2]{0,1:T(2,128)}, u32[]{:S(2)}) copy-start(f32[128,2]{0,1:T(2,128)} %param.20) | copy-start | bytes 3076
  0.7 23.8 %copy-start.8 = (s32[128,2]{0,1:T(2,128)S(1)}, s32[128,2]{0,1:T(2,128)}, u32[]{:S(2)}) copy-start(s32[128,2]{0,1:T(2,128)} %param.19) | copy-start | bytes 3076
  0.7 62.6 %copy-start.4 = (bf16[128,96]{0,1:T(8,128)(2,1)S(1)}, bf16[128,96]{0,1:T(8,128)(2,1)}, u32[]{:S(2)}) copy-start(bf16[128,96]{0,1:T(8,128)(2,1)} %param.11) | copy-start | bytes 73732
  2.7 19.0 %all-to-all-start = ((bf16[16,144,128]{2,1,0:T(8,128)(2,1)}), bf16[16,144,128]{2,1,0:T(8,128)(2,1)S(1)}, u32[]{:S(2)}, u32[]{:S(2)}) async-start(bf16[16,144,128]{2,1,0:T(8,128)(2,1)} %shard_map.146), calls=%async_computation | async-start | bytes 1179648 | tf_op jit(solution)/shard_map/all_to_all | solution.py:329
  10.6 1.1 copy-start
  11.8 0.7 copy-start.6
  13.5 11.2 %collective-permute-start.1 = (bf16[16,96,128]{2,1,0:T(8,128)(2,1)S(1)}, bf16[16,96,128]{2,1,0:T(8,128)(2,1)S(1)}, u32[]{:S(2)}, u32[]{:S(2)}) collective-permute-start(bf16[16,96,128]{2,1,0:T(8,128)(2,1)S(1)} %get-tuple-element.33), channel_id=1, source_target_pairs={{0,1},{1,0},{2,3},{3,2},{4,5},{5,4},{6,7},{7,6},{8,9},{9,8},{10,11... | collective-permute-start | bytes 1179656 | tf_op jit(solution)/shard_map/ppermute | solution.py:339
  22.5 3.1 %collective-permute-start = (bf16[128,128]{1,0:T(8,128)(2,1)S(1)}, bf16[128,128]{1,0:T(8,128)(2,1)S(1)}, u32[]{:S(2)}, u32[]{:S(2)}) collective-permute-start(bf16[128,128]{1,0:T(8,128)(2,1)S(1)} %get-tuple-element.31.heads), channel_id=1, source_target_pairs={{0,1},{1,0},{2,3},{3,2},{4,5},{5,4},{6,7},{7,6},{8,9},{9,8},{10,11... | collective-permute-start | bytes 98312 | tf_op jit(solution)/shard_map/ppermute | solution.py:352
  102.5 25.0 %copy-start.2 = (bf16[1,3072,384]{2,1,0:T(8,128)(2,1)S(1)}, bf16[1,3072,384]{2,1,0:T(8,128)(2,1)}, u32[]{:S(2)}) copy-start(bf16[1,3072,384]{2,1,0:T(8,128)(2,1)} %param.17) | copy-start | bytes 7077892
  102.5 25.0 %copy-start.3 = (bf16[1,384,3072]{2,1,0:T(8,128)(2,1)S(1)}, bf16[1,384,3072]{2,1,0:T(8,128)(2,1)}, u32[]{:S(2)}) copy-start(bf16[1,384,3072]{2,1,0:T(8,128)(2,1)} %param.18) | copy-start | bytes 7077892
  156.1 67.3 %copy-start.1 = (bf16[128,3072]{1,0:T(8,128)(2,1)S(1)}, bf16[128,3072]{1,0:T(8,128)(2,1)}, u32[]{:S(2)}) copy-start(bf16[128,3072]{1,0:T(8,128)(2,1)} %w_out.3) | copy-start | bytes 2359300
  224.9 15.8 %all-to-all-start.8 = ((bf16[16,128,128]{2,1,0:T(8,128)(2,1)}), bf16[16,128,128]{2,1,0:T(8,128)(2,1)S(1)}, u32[]{:S(2)}, u32[]{:S(2)}) async-start(bf16[16,128,128]{2,1,0:T(8,128)(2,1)} %get-tuple-element.47), calls=%async_computation.8 | async-start | bytes 1048576 | tf_op jit(solution)/shard_map/all_to_all | solution.py:397
